TPU v7x, 32 devices: a whole 2x2x4 slice. The times are simulated.
32 devices in a mesh: dom: 8 (over z, y), tile: 4 (over x, core).
Axes of the slice: x: 2, y: 2, z: 4, core: 2. Of those that a mesh axis runs over, the one named last changes fastest.
Arguments:
- features: bfloat16 [16384, 256], P(('dom', 'tile')), may hold values from -6 to 6
- grad_out: bfloat16 [16384, 256], P(('dom', 'tile')), may hold values from -6 to 6
- self_weight: bfloat16 [256, 256], replicated, may hold values from -0.375 to 0.375
- neigh_weight: bfloat16 [256, 256], replicated, may hold values from -0.375 to 0.375
- edge_tiles: bfloat16 [2304, 128, 128], P(('dom', 'tile')), may hold values from 0 to 1.5, as said below
- tile_dst: int32 [2304], P(('dom', 'tile')), may hold values from 0 to 15
- tile_src: int32 [2304], P(('dom', 'tile')), may hold values from 0 to 25
- halo_send: int32 [8, 1024], P('dom'), may hold values from 0 to 2047
- hub_ids: int32 [256], P('dom'), may hold values from 0 to 2047
Outputs:
- activated: bfloat16 [16384, 256], P(('dom', 'tile'))
- grad_features: bfloat16 [16384, 256], P(('dom', 'tile'))
- grad_self_weight: float32 [256, 256], replicated
- grad_neigh_weight: float32 [256, 256], replicated
Inputs may be any that keep to these rules, and one draw needn't show every extreme that they name: `edge_tiles`: each entry is zero or an edge weight of 0.3 or more.
All inputs are finite; a program needn't handle non-finite values.
Results may differ from a plain program's by a relative error of at most 0.014.
Values may be sent and summed in bfloat16 or wider, within the bound.
A program may use at most 64 MiB of HBM per device.

v0:
```python
import jax
import jax.numpy as jnp
from jax import lax
from jax.sharding import PartitionSpec as P


def block_onehot(indices, number):
    return (indices[None, :] == jnp.arange(number, dtype=jnp.int32)[:, None]).astype(jnp.float32)


def on_device(
    features,
    grad_out,
    self_weight,
    neigh_weight,
    edge_tiles,
    tile_dst,
    tile_src,
    halo_send,
    hub_ids,
):
    domains = lax.axis_size("dom")
    groups = lax.axis_size("tile")
    quarter = features.shape[0]
    columns = features.shape[1]
    tile_size = edge_tiles.shape[1]
    halo_total = halo_send.shape[1]
    per_peer = halo_total // domains
    whole_rows = lax.all_gather(features, "tile", axis=0, tiled=True)
    vertices = whole_rows.shape[0]
    outgoing = whole_rows[halo_send[0]].reshape(domains, per_peer, columns)
    own_hubs = whole_rows[hub_ids]
    width = outgoing.shape[2]
    halo_rows = lax.all_to_all(outgoing, "dom", split_axis=0, concat_axis=0, tiled=True).reshape(
        halo_total, width
    )
    hub_rows = lax.all_gather(own_hubs, "dom", axis=0, tiled=True)
    boundary = jnp.concatenate([halo_rows, hub_rows], axis=0)
    source = jnp.concatenate([whole_rows, boundary], axis=0)
    src_rows = source.shape[0]
    src_blocks = src_rows // tile_size
    dst_blocks = vertices // tile_size
    picked = source.reshape(src_blocks, tile_size, columns)[tile_src]
    products = jnp.einsum("tij,tjf->tif", edge_tiles, picked, preferred_element_type=jnp.float32)
    into_dest = block_onehot(tile_dst, dst_blocks)
    partial_sum = jnp.einsum(
        "dt,tif->dif", into_dest, products, precision=lax.Precision.HIGHEST
    ).reshape(vertices, columns)
    row_weight = jnp.sum(edge_tiles, axis=2, dtype=jnp.float32)
    partial_degree = jnp.dot(into_dest, row_weight, precision=lax.Precision.HIGHEST).reshape(
        vertices
    )
    summed, degree = (
        lax.psum_scatter(
            partial_sum.astype(jnp.bfloat16), "tile", scatter_dimension=0, tiled=True
        ).astype(jnp.float32),
        lax.psum_scatter(
            partial_degree.astype(jnp.bfloat16), "tile", scatter_dimension=0, tiled=True
        ).astype(jnp.float32),
    )
    divisor = jnp.maximum(degree, 1.0)
    mean_rows = (summed / divisor[:, None]).astype(jnp.bfloat16)
    hidden = jnp.dot(features, self_weight, preferred_element_type=jnp.float32) + jnp.dot(
        mean_rows, neigh_weight, preferred_element_type=jnp.float32
    )
    activated = jax.nn.silu(hidden).astype(jnp.bfloat16)
    sigmoid_h = jax.nn.sigmoid(hidden)
    grad_hidden = (
        grad_out.astype(jnp.float32) * sigmoid_h * (1.0 + hidden * (1.0 - sigmoid_h))
    ).astype(jnp.bfloat16)
    self_term = jnp.einsum("nf,nh->fh", features, grad_hidden, preferred_element_type=jnp.float32)
    neigh_term = jnp.einsum("nf,nh->fh", mean_rows, grad_hidden, preferred_element_type=jnp.float32)
    grad_self_sum, grad_neigh_sum = lax.psum((self_term, neigh_term), ("dom", "tile"))
    inv_root = 1.0 / (quarter * groups * domains) ** 0.5
    grad_mean = lax.dot_general(
        grad_hidden, neigh_weight, (((1,), (1,)), ((), ())), preferred_element_type=jnp.float32
    )
    grad_mean_b = (grad_mean / divisor[:, None]).astype(jnp.bfloat16)
    grad_whole = lax.all_gather(grad_mean_b, "tile", axis=0, tiled=True)
    dst_pick = grad_whole.reshape(dst_blocks, tile_size, columns)[tile_dst]
    back_prod = jnp.einsum("tij,tif->tjf", edge_tiles, dst_pick, preferred_element_type=jnp.float32)
    into_source = block_onehot(tile_src, src_blocks)
    partial_src = jnp.einsum(
        "st,tjf->sjf", into_source, back_prod, precision=lax.Precision.HIGHEST
    ).reshape(src_rows, columns)
    grad_local = lax.psum_scatter(
        partial_src[:vertices].astype(jnp.bfloat16), "tile", scatter_dimension=0, tiled=True
    ).astype(jnp.float32)
    remote = lax.psum(partial_src[vertices:].astype(jnp.bfloat16), "tile").astype(jnp.float32)
    halo_grad = remote[:halo_total].reshape(domains, per_peer, width)
    hub_grad = remote[halo_total:]
    halo_back = (
        lax.all_to_all(
            halo_grad.astype(jnp.bfloat16), "dom", split_axis=0, concat_axis=0, tiled=True
        )
        .astype(halo_grad.dtype)
        .reshape(halo_total, width)
    )
    hub_back = lax.psum_scatter(hub_grad, "dom", scatter_dimension=0, tiled=True)
    spread = jnp.zeros((vertices, width), jnp.float32).at[halo_send[0]].add(halo_back)
    spread = spread.at[hub_ids].add(hub_back)
    own_spread = lax.dynamic_slice_in_dim(spread, lax.axis_index("tile") * quarter, quarter, 0)
    grad_features = (
        lax.dot_general(
            grad_hidden, self_weight, (((1,), (1,)), ((), ())), preferred_element_type=jnp.float32
        )
        + grad_local
        + own_spread
    )
    return (
        activated,
        grad_features.astype(jnp.bfloat16),
        grad_self_sum * inv_root,
        grad_neigh_sum * inv_root,
    )


def solution(mesh):
    return jax.shard_map(
        on_device,
        mesh=mesh,
        in_specs=(
            P(("dom", "tile"), None),
            P(("dom", "tile"), None),
            P(),
            P(),
            P(("dom", "tile"), None, None),
            P(("dom", "tile")),
            P(("dom", "tile")),
            P("dom", None),
            P("dom"),
        ),
        out_specs=(P(("dom", "tile"), None), P(("dom", "tile"), None), P(), P()),
        check_vma=False,
    )
```

profile of v0, /device:TPU:0, one launch (start us, length us, event | category | flops | bytes accessed | tf_op | source)
XLA Modules:
  0.0 453.9 jit_solution(10285785023682862956)
XLA Ops:
  8.6 20.4 %all-gather.4.cloned.1.call-done = bf16[2048,256]{1,0:T(8,128)(2,1)} async-done(((bf16[512,256]{1,0:T(8,128)(2,1)}), bf16[2048,256]{1,0:T(8,128)(2,1)}) %all-gather.4.cloned.1.call-update) | async-done | bytes 1048592 | tf_op jit(solution)/shard_map/all_gather | solution.py:29
  29.1 6.0 %gather_fusion = bf16[1024,256]{1,0:T(8,128)(2,1)} fusion(bf16[2048,256]{1,0:T(8,128)(2,1)} %all-gather.4.cloned.1.call-done, s32[1024]{0:T(1024)S(1)} %broadcast_clamp_fusion), kind=kCustom, calls=%fused_computation | custom fusion | bytes 1052672 | tf_op jit(solution)/shard_map/gather | solution.py:31
  35.1 5.5 %all-to-all-start = ((bf16[8,128,256]{2,1,0:T(8,128)(2,1)}), bf16[8,128,256]{2,1,0:T(8,128)(2,1)S(1)}, u32[]{:S(2)}, u32[]{:S(2)}) async-start(bf16[8,128,256]{2,1,0:T(8,128)(2,1)} %bitcast.3), calls=%async_computation | async-start | bytes 1048576 | tf_op jit(solution)/shard_map/all_to_all | solution.py:34
  41.4 36.8 %all-gather = bf16[256,256]{1,0:T(8,128)(2,1)S(1)} all-gather(bf16[32,256]{1,0:T(8,128)(2,1)S(1)} %gather_fusion.1), channel_id=2, replica_groups=mesh['dom'=8,'tile'=4] {'dom'}, dimensions={0}, use_global_device_ids=true | all-gather | bytes 147456 | tf_op jit(solution)/shard_map/all_gather | solution.py:37
  78.3 5.6 %gather_fusion.2 = bf16[72,128,256]{2,1,0:T(8,128)(2,1)} fusion(bf16[26,128,256]{2,1,0:T(8,128)(2,1)S(1)} %bitcast.45, s32[1024]{0:T(1024)S(1)} %pad_clamp_fusion.1), kind=kCustom, calls=%fused_computation.2 | custom fusion | bytes 9437472 | tf_op jit(solution)/shard_map/gather | solution.py:43
  83.9 8.2 %convolution_bitcast_fusion.1 = f32[72,128,256]{1,2,0:T(8,128)} fusion(bf16[72,128,256]{2,1,0:T(8,128)(2,1)} %gather_fusion.2, bf16[72,128,128]{2,1,0:T(8,128)(2,1)} %param.13), kind=kOutput, calls=%fused_computation.8 | convolution fusion | flops 603979776 | bytes 16515072 | tf_op jit(solution)/shard_map/tij,tjf->tif/dot_general | solution.py:44
  92.1 9.6 %copy.33 = f32[72,128,256]{2,0,1:T(8,128)} copy(f32[72,128,256]{1,2,0:T(8,128)} %convolution_bitcast_fusion.1) | data formatting | bytes 18874368 | tf_op jit(solution)/shard_map/tij,tjf->tif/dot_general | solution.py:44
  101.7 6.9 %convolution_convert_fusion.1 = bf16[16,128,256]{2,0,1:T(8,128)(2,1)S(1)} fusion(f32[72,128,256]{2,0,1:T(8,128)} %copy.33, s32[72]{0:T(128)S(1)} %copy-done.8), kind=kOutput, calls=%fused_computation.11 | convolution fusion | flops 453510272 | bytes 10486048 | tf_op jit(solution)/shard_map/dt,tif->dif/dot_general | solution.py:46
  112.2 5.9 %all-reduce = bf16[2048]{0:T(1024)(128)(2,1)S(1)} all-reduce(bf16[2048]{0:T(1024)(128)(2,1)S(1)} %fusion.3), channel_id=4, replica_groups=mesh['dom'=8,'tile'=4] {'tile'}, use_global_device_ids=true, to_apply=%region_2.0.clone | all-reduce | flops 2048 | bytes 8192
  118.4 13.0 %reduce-scatter.4.cloned.1.call-done = bf16[512,256]{1,0:T(8,128)(2,1)} async-done(((bf16[2048,256]{1,0:T(8,128)(2,1)}), bf16[512,256]{1,0:T(8,128)(2,1)}) %reduce-scatter.4.cloned.1.call-update) | async-done | bytes 262160 | tf_op jit(solution)/shard_map/reduce_scatter | solution.py:54
  131.4 2.2 multiply_convert_fusion
  134.9 16.6 %all-gather.6.cloned.1.call-done = bf16[2048,256]{1,0:T(8,128)(2,1)} async-done(((bf16[512,256]{1,0:T(8,128)(2,1)}), bf16[2048,256]{1,0:T(8,128)(2,1)}) %all-gather.6.cloned.1.call-update) | async-done | bytes 1048592 | tf_op jit(solution)/shard_map/all_gather | solution.py:79
  151.5 6.8 %gather_fusion.3 = bf16[72,128,256]{2,1,0:T(8,128)(2,1)} fusion(bf16[16,128,256]{2,1,0:T(8,128)(2,1)} %bitcast.46, s32[1024]{0:T(1024)S(1)} %pad_clamp_fusion), kind=kCustom, calls=%fused_computation.3 | custom fusion | bytes 9437472 | tf_op jit(solution)/shard_map/gather | solution.py:80
  158.3 7.4 %convolution_bitcast_fusion = f32[72,128,256]{1,2,0:T(8,128)} fusion(bf16[72,128,256]{2,1,0:T(8,128)(2,1)} %gather_fusion.3, bf16[72,128,128]{2,1,0:T(8,128)(2,1)S(1)} %copy-done.3), kind=kOutput, calls=%fused_computation.7 | convolution fusion | flops 603979776 | bytes 16515072 | tf_op jit(solution)/shard_map/tij,tif->tjf/dot_general | solution.py:81
  165.7 9.6 %copy.36 = f32[72,128,256]{2,0,1:T(8,128)} copy(f32[72,128,256]{1,2,0:T(8,128)} %convolution_bitcast_fusion) | data formatting | bytes 18874368 | tf_op jit(solution)/shard_map/tij,tif->tjf/dot_general | solution.py:81
  175.4 7.7 %convolution_convert_fusion = bf16[26,128,256]{2,0,1:T(8,128)(2,1)S(1)} fusion(f32[72,128,256]{2,0,1:T(8,128)} %copy.36, s32[72]{0:T(128)S(1)} %copy-done.10), kind=kOutput, calls=%fused_computation.9 | convolution fusion | flops 736954176 | bytes 11141408 | tf_op jit(solution)/shard_map/st,tjf->sjf/dot_general | solution.py:83
  186.4 31.8 %all-reduce.5.cloned.1.call-done = bf16[1280,256]{1,0:T(8,128)(2,1)} async-done(((bf16[1280,256]{1,0:T(8,128)(2,1)}), bf16[1280,256]{1,0:T(8,128)(2,1)}) %all-reduce.5.cloned.1.call-update) | async-done | bytes 655376 | tf_op jit(solution)/shard_map/psum | solution.py:89
  222.2 5.7 %all-to-all-start.1 = ((bf16[8,128,256]{2,1,0:T(8,128)(2,1)}), bf16[8,128,256]{2,1,0:T(8,128)(2,1)S(1)}, u32[]{:S(2)}, u32[]{:S(2)}) async-start(bf16[8,128,256]{2,1,0:T(8,128)(2,1)} %bitcast.14), calls=%async_computation.3 | async-start | bytes 1048576 | tf_op jit(solution)/shard_map/all_to_all | solution.py:93
  227.9 126.8 %all-reduce.7.cloned.1.call-done = (f32[256,256]{0,1:T(8,128)}, f32[256,256]{0,1:T(8,128)}) async-done(((f32[256,256]{0,1:T(8,128)}, f32[256,256]{0,1:T(8,128)}), (f32[256,256]{0,1:T(8,128)}, f32[256,256]{0,1:T(8,128)})) %all-reduce.7.cloned.1.call-update) | async-done | bytes 524304 | tf_op jit(solution)/shard_map/psum | solution.py:73
  357.5 6.6 %scatter_custom_fusion = f32[2048,256]{1,0:T(8,128)S(1)} fusion(s32[1024]{0:T(1024)S(1)} %bitcast.53, bf16[1024,256]{1,0:T(8,128)(2,1)S(1)} %bitcast.50, f32[]{:T(128)} %constant.12.clone.1), kind=kCustom, calls=%fused_computation.21 | custom fusion | flops 524288 | bytes 2621444 | tf_op jit(solution)/shard_map/scatter-add | solution.py:100
  364.1 54.6 %reduce-scatter.8.cloned.1.call-done = f32[32,256]{1,0:T(8,128)} async-done(((f32[256,256]{1,0:T(8,128)}), f32[32,256]{1,0:T(8,128)}) %reduce-scatter.8.cloned.1.call-update) | async-done | bytes 32784 | tf_op jit(solution)/shard_map/reduce_scatter | solution.py:99
  418.7 1.8 scatter_fusion
  420.5 24.7 %reduce-scatter.6.cloned.1.call-done = bf16[512,256]{1,0:T(8,128)(2,1)} async-done(((bf16[2048,256]{1,0:T(8,128)(2,1)}), bf16[512,256]{1,0:T(8,128)(2,1)}) %reduce-scatter.6.cloned.1.call-update) | async-done | bytes 262160 | tf_op jit(solution)/shard_map/reduce_scatter | solution.py:86
  445.2 1.9 fusion.1
  (72 shorter events, 16.6 us)
Async XLA Ops:
  7.2 124.3 %copy-start = (bf16[256,256]{1,0:T(8,128)(2,1)S(1)}, bf16[256,256]{1,0:T(8,128)(2,1)}, u32[]{:S(2)}) copy-start(bf16[256,256]{1,0:T(8,128)(2,1)} %param.12) | copy-start | bytes 393220
  7.2 33.5 %copy-start.12 = (s32[32]{0:T(128)S(1)}, s32[32]{0:T(128)}, u32[]{:S(2)}) copy-start(s32[32]{0:T(128)} %param.17) | copy-start | bytes 388
  7.2 33.5 %copy-start.9 = (s32[72]{0:T(128)S(1)}, s32[72]{0:T(128)}, u32[]{:S(2)}) copy-start(s32[72]{0:T(128)} %param.15) | copy-start | bytes 868
  7.2 21.8 %all-gather.4.cloned.1.call-start = ((), (), s32[]{:S(2)}) async-start(), calls=%async_computation.5 | async-start | bytes 1310720 | tf_op jit(solution)/shard_map/all_gather | solution.py:29
  29.1 11.7 %copy-start.2 = (bf16[2048,256]{1,0:T(8,128)(2,1)S(1)}, bf16[2048,256]{1,0:T(8,128)(2,1)}, u32[]{:S(2)}) copy-start(bf16[2048,256]{1,0:T(8,128)(2,1)} %all-gather.4.cloned.1.call-done) | copy-start | bytes 3145732
  35.1 43.1 %all-to-all-start = ((bf16[8,128,256]{2,1,0:T(8,128)(2,1)}), bf16[8,128,256]{2,1,0:T(8,128)(2,1)S(1)}, u32[]{:S(2)}, u32[]{:S(2)}) async-start(bf16[8,128,256]{2,1,0:T(8,128)(2,1)} %bitcast.3), calls=%async_computation | async-start | bytes 1048576 | tf_op jit(solution)/shard_map/all_to_all | solution.py:34
  40.6 90.8 %reduce-scatter.4.cloned.1.call-start = ((), (), s32[]{:S(2)}) async-start(), calls=%async_computation.6 | async-start | bytes 1310720 | tf_op jit(solution)/shard_map/reduce_scatter | solution.py:54
  92.1 9.6 %copy-start.8 = (s32[72]{0:T(128)S(1)}, s32[72]{0:T(128)}, u32[]{:S(2)}) copy-start(s32[72]{0:T(128)} %param.14) | copy-start | bytes 868
  101.7 8.4 %copy-start.13 = (u32[32]{0:T(128)S(1)}, u32[32]{0:T(128)}, u32[]{:S(2)}) copy-start(u32[32]{0:T(128)} %constant.8) | copy-start | bytes 388
  108.7 2.7 copy-start.3
  108.7 9.5 %copy-start.4 = (bf16[512,256]{1,0:T(8,128)(2,1)S(1)}, bf16[512,256]{1,0:T(8,128)(2,1)}, u32[]{:S(2)}) copy-start(bf16[512,256]{1,0:T(8,128)(2,1)} %param.9) | copy-start | bytes 786436
  108.7 9.5 %copy-start.6 = (bf16[256,256]{1,0:T(8,128)(2,1)S(1)}, bf16[256,256]{1,0:T(8,128)(2,1)}, u32[]{:S(2)}) copy-start(bf16[256,256]{1,0:T(8,128)(2,1)} %param.11) | copy-start | bytes 393220
  110.1 41.4 %all-gather.6.cloned.1.call-start = ((), (), s32[]{:S(2)}) async-start(), calls=%async_computation.7 | async-start | bytes 1310720 | tf_op jit(solution)/shard_map/all_gather | solution.py:79
  134.6 83.6 %all-reduce.5.cloned.1.call-start = ((), (), s32[]{:S(2)}) async-start(), calls=%async_computation.9 | async-start | bytes 1310720 | tf_op jit(solution)/shard_map/psum | solution.py:89
  165.7 9.6 %copy-start.10 = (s32[72]{0:T(128)S(1)}, s32[72]{0:T(128)}, u32[]{:S(2)}) copy-start(s32[72]{0:T(128)} %param.15) | copy-start | bytes 868
  183.1 2.2 copy-start.11
  184.2 170.5 %all-reduce.7.cloned.1.call-start = ((), (), s32[]{:S(2)}) async-start(), calls=%async_computation.11 | async-start | bytes 1048576 | tf_op jit(solution)/shard_map/psum | solution.py:73
  186.4 232.3 %reduce-scatter.8.cloned.1.call-start = ((), (), s32[]{:S(2)}) async-start(), calls=%async_computation.10 | async-start | bytes 294912 | tf_op jit(solution)/shard_map/reduce_scatter | solution.py:99
  219.8 225.3 %reduce-scatter.6.cloned.1.call-start = ((), (), s32[]{:S(2)}) async-start(), calls=%async_computation.8 | async-start | bytes 1310720 | tf_op jit(solution)/shard_map/reduce_scatter | solution.py:86
  220.0 1.4 copy-start.5
  222.2 223.0 %copy-start.7 = (bf16[256,256]{1,0:T(8,128)(2,1)S(1)}, bf16[256,256]{1,0:T(8,128)(2,1)}, u32[]{:S(2)}) copy-start(bf16[256,256]{1,0:T(8,128)(2,1)} %param.11) | copy-start | bytes 393220
  222.2 135.2 %all-to-all-start.1 = ((bf16[8,128,256]{2,1,0:T(8,128)(2,1)}), bf16[8,128,256]{2,1,0:T(8,128)(2,1)S(1)}, u32[]{:S(2)}, u32[]{:S(2)}) async-start(bf16[8,128,256]{2,1,0:T(8,128)(2,1)} %bitcast.14), calls=%async_computation.3 | async-start | bytes 1048576 | tf_op jit(solution)/shard_map/all_to_all | solution.py:93
  227.9 219.2 %copy-start.1 = (bf16[256,256]{1,0:T(8,128)(2,1)S(1)}, bf16[256,256]{1,0:T(8,128)(2,1)}, u32[]{:S(2)}) copy-start(bf16[256,256]{1,0:T(8,128)(2,1)} %param.12) | copy-start | bytes 393220
Sparse Core Ops, SparseCore 0:
  9.6 19.4 all-gather.3
  110.2 21.1 reduce-scatter.3
  134.7 16.7 all-gather.5
  184.4 33.7 all-reduce.4
  225.0 129.7 all-reduce.6
  358.5 60.1 reduce-scatter.7
  421.2 23.9 reduce-scatter.5
where the time goes:
time: 455 us; the launch traced here: 454 us
  waiting for transfers between devices  289 us (64%)
  local copies, waits for them, and re-layouts  45.4 us (10%)
  blocking collectives  42.8 us (9%)
  matrix products  37.7 us (8%)
  between operations  15 us (3%)
  other arithmetic  12.7 us (3%)
  starting transfers between devices  11.6 us (3%)
    psum x1, waiting for transfers between devices, on_device(): lax.psum((self_term, neigh_term), ('dom', 'tile'))  127 us
    reduce_scatter x1, waiting for transfers between devices, on_device(): lax.psum_scatter(hub_grad, 'dom', scatter_dimension=0, tiled=True)  54.6 us
    all_gather x1, blocking collectives, on_device(): hub_rows = lax.all_gather(own_hubs, 'dom', axis=0, tiled=True)  36.8 us
    psum x1, waiting for transfers between devices, on_device(): lax.psum(partial_src[vertices:].astype(jnp.bfloat16), 'tile')  31.8 us
    reduce_scatter x1, waiting for transfers between devices, on_device(): lax.psum_scatter(partial_src[:vertices].astype(jnp.bfloat16), 'tile', sca...  24.7 us
    all_gather x1, waiting for transfers between devices, on_device(): whole_rows = lax.all_gather(features, 'tile', axis=0, tiled=True)  20.4 us
    all_gather x1, waiting for transfers between devices, on_device(): grad_whole = lax.all_gather(grad_mean_b, 'tile', axis=0, tiled=True)  16.6 us
    reduce_scatter x1, waiting for transfers between devices, on_device(): lax.psum_scatter(partial_sum.astype(jnp.bfloat16), 'tile', scatter_dimens...  13 us
  transfers between devices with their start and end apart: 9, of which 7 were waited for; matrix products, arithmetic and copies ran while one was open for 4% of the time, Pallas kernels for 0%

commit v1 on v0

v1 whole, which is shorter than its diff:
```python
import functools

import jax
import jax.numpy as jnp
from jax import lax
from jax.experimental import pallas as pl
from jax.experimental.pallas import tpu as pltpu
from jax.sharding import PartitionSpec as P

BF = jnp.bfloat16
F32 = jnp.float32
MESH = pl.DeviceIdType.MESH
VMEM = pl.BlockSpec(memory_space=pltpu.VMEM)
SMEM = pl.BlockSpec(memory_space=pltpu.SMEM)
ANY = pl.BlockSpec(memory_space=pl.ANY)
LIMIT = 40 * 1024 * 1024
NT = (((1,), (1,)), ((), ()))
TN = (((0,), (0,)), ((), ()))


def places(domains):
    me = lax.axis_index("dom")
    t = lax.axis_index("tile")
    core = t + 1 - 2 * lax.rem(t, 2)
    across = lax.rem(t + 2, 4)
    diagonal = lax.rem(core + 2, 4)

    def slots(who):
        first = lax.rem(who + 4 * domains - me, 4)
        return lambda i: first + 4 * i

    return me, t, core, across, diagonal, slots


def remote(src, dst, send, recv, **device):
    return pltpu.make_async_remote_copy(
        src_ref=src,
        dst_ref=dst,
        send_sem=send,
        recv_sem=recv,
        device_id=device,
        device_id_type=MESH,
    )


def greet(me, peers, others, count):
    barrier = pltpu.get_barrier_semaphore()
    for peer in peers:
        pl.semaphore_signal(barrier, inc=1, device_id={"tile": peer}, device_id_type=MESH)
    for i in range(count):
        there = others(i)

        @pl.when(there != me)
        def _():
            pl.semaphore_signal(barrier, inc=1, device_id={"dom": there}, device_id_type=MESH)

    own = jnp.where(lax.rem(others(0) + 4 * count - me, 4) == 0, 1, 0) if count else 0
    pl.semaphore_wait(barrier, len(peers) + count - own)


def each(count, body):
    if count <= 4:
        for i in range(count):
            body(i)
    else:

        def step(i, carry):
            body(i)
            return carry

        lax.fori_loop(0, count, step, 0)


def dom_send(count, me, own_slots, pairs):
    def body(i):
        there = own_slots(i)
        for staged, landing, send, recv in pairs:

            @pl.when(there != me)
            def _():
                remote(staged.at[i], landing.at[me], send.at[i], recv.at[me], dom=there).start()

            @pl.when(there == me)
            def _():
                landing[me] = staged[i]

    each(count, body)


def dom_gather(count, me, t, core, across, diagonal, slots, pairs, forward):
    mine, theirs = slots(t), slots(across)

    def first(i):
        there = mine(i)
        for (staged, landing, send, recv), (fcore, facross) in zip(pairs, forward):

            @pl.when(there != me)
            def _():
                copy = remote(staged.at[i], landing.at[there], send.at[i], recv.at[there], dom=there)
                copy.wait_send()
                copy.wait_recv()

            spot = landing.at[there]
            remote(spot, spot, facross.at[there], recv.at[there], tile=across).start()
            remote(spot, spot, fcore.at[there], recv.at[there], tile=core).start()

    each(count, first)

    def second(i):
        there = theirs(i)
        for (staged, landing, send, recv), (fcore, facross) in zip(pairs, forward):
            spot = landing.at[there]
            remote(spot, spot, facross.at[there], recv.at[there], tile=across).wait_recv()
            remote(spot, spot, fcore.at[there], recv.at[there], tile=core).start()

    each(count, second)

    def third(i):
        for (staged, landing, send, recv), (fcore, facross) in zip(pairs, forward):
            for who in (core, diagonal):
                there = slots(who)(i)
                spot = landing.at[there]
                remote(spot, spot, fcore.at[there], recv.at[there], tile=core).wait_recv()
            for there, sem, peer in (
                (mine(i), facross, across),
                (mine(i), fcore, core),
                (theirs(i), fcore, core),
            ):
                spot = landing.at[there]
                remote(spot, spot, sem.at[there], recv.at[there], tile=peer).wait_send()

    each(count, third)


def tile_gather_start(src, out, t, core, across, send, recv):
    remote(src, out.at[t], send.at[0], recv.at[t], tile=across).start()
    remote(src, out.at[t], send.at[1], recv.at[t], tile=core).start()


def tile_gather_middle(out, core, across, send, recv):
    spot = out.at[across]
    remote(spot, spot, send.at[0], recv.at[across], tile=across).wait_recv()
    remote(spot, spot, send.at[2], recv.at[across], tile=core).start()


def tile_gather_end(src, out, core, across, diagonal, send, recv):
    for who in (core, diagonal):
        remote(out.at[who], out.at[who], send.at[1], recv.at[who], tile=core).wait_recv()
    remote(src, out.at[core], send.at[0], recv.at[core], tile=across).wait_send()
    remote(src, out.at[core], send.at[1], recv.at[core], tile=core).wait_send()
    remote(out.at[across], out.at[across], send.at[2], recv.at[core], tile=core).wait_send()


def collect_kernel(
    domains,
    feat,
    halo_ids,
    hub_ids,
    local,
    halo,
    hub,
    staged_halo,
    staged_hub,
    tile_send,
    tile_recv,
    halo_send,
    hub_send,
    halo_recv,
    hub_recv,
    halo_core,
    halo_across,
    hub_core,
    hub_across,
):
    count = domains // 4
    me, t, core, across, diagonal, slots = places(domains)
    mine = slots(t)
    quarter = feat.shape[0]
    greet(me, (core, across, diagonal), mine, count)
    tile_gather_start(feat, local, t, core, across, tile_send, tile_recv)
    local[t] = feat[...]
    tile_gather_middle(local, core, across, tile_send, tile_recv)
    tile_gather_end(feat, local, core, across, diagonal, tile_send, tile_recv)

    def rows(ids):
        total = None
        for part in range(4):
            spot = lax.broadcasted_iota(jnp.int32, (quarter, ids.shape[1]), 0) + part * quarter
            chosen = (spot == ids).astype(F32).astype(BF)
            term = lax.dot_general(chosen, local[part], TN, preferred_element_type=F32)
            total = term if total is None else total + term
        return total.astype(BF)

    own_hubs = rows(hub_ids[...])

    def body(i):
        staged_hub[i] = own_hubs
        staged_halo[i] = rows(halo_ids[mine(i)])

    each(count, body)
    pairs = ((staged_halo, halo, halo_send, halo_recv), (staged_hub, hub, hub_send, hub_recv))
    forward = ((halo_core, halo_across), (hub_core, hub_across))
    dom_send(count, me, mine, pairs)
    dom_gather(count, me, t, core, across, diagonal, slots, pairs, forward)


def forward_kernel(tiles, dst, src, local, halo, hub, out, deg, source, acc, sems):
    nl, nh = local.shape[0], halo.shape[0]
    copies = [
        pltpu.make_async_copy(local, source.at[pl.ds(0, nl)], sems.at[0]),
        pltpu.make_async_copy(halo, source.at[pl.ds(nl, nh)], sems.at[1]),
        pltpu.make_async_copy(hub, source.at[pl.ds(nl + nh, hub.shape[0])], sems.at[2]),
    ]
    for copy in copies:
        copy.start()
    acc[...] = jnp.zeros_like(acc)
    deg[...] = jnp.zeros_like(deg)
    ones = jnp.ones((8, tiles.shape[2]), BF)
    for copy in copies:
        copy.wait()
    step = 4

    def body(k, carry):
        found = []
        for i in range(step):
            j = k * step + i
            e = tiles[j]
            found.append(
                (
                    dst[j],
                    jnp.dot(e, source[src[j]], preferred_element_type=F32),
                    lax.dot_general(ones, e, NT, preferred_element_type=F32),
                )
            )
        for d, product, weight in found:
            acc[d] += product
            deg[d] += weight
        return carry

    lax.fori_loop(0, tiles.shape[0] // step, body, 0)
    out[...] = acc[...].astype(BF)


def backward_kernel(tiles, dst, src, grad, local, halo, hub, acc):
    nl, nh = local.shape[0], halo.shape[0]
    acc[...] = jnp.zeros_like(acc)
    step = 4

    def body(k, carry):
        found = []
        for i in range(step):
            j = k * step + i
            found.append(
                (
                    src[j],
                    lax.dot_general(tiles[j], grad[dst[j]], TN, preferred_element_type=F32),
                )
            )
        for s, product in found:
            acc[s] += product
        return carry

    lax.fori_loop(0, tiles.shape[0] // step, body, 0)
    local[...] = acc[pl.ds(0, nl)].astype(BF)
    halo[...] = acc[pl.ds(nl, nh)].astype(BF)
    hub[...] = acc[pl.ds(nl + nh, hub.shape[0])].astype(BF)


def pair_send(partial, landing, send, recv, core, diagonal):
    remote(partial.at[diagonal], landing.at[1], send.at[1], recv.at[1], tile=core).start()
    remote(partial.at[core], landing.at[0], send.at[0], recv.at[0], tile=core).start()


def dense_kernel(
    domains,
    partial,
    deg,
    feat,
    grad_out,
    self_weight,
    neigh_weight,
    activated,
    grad_hidden,
    grad_all,
    self_term,
    neigh_term,
    landing,
    other,
    passing,
    deg_in,
    mine_b,
    pair_sems,
    pair_recv,
    cross_sem,
    cross_recv,
    deg_send,
    deg_recv,
    tile_send,
    tile_recv,
):
    me, t, core, across, diagonal, slots = places(domains)
    greet(me, (core, across, diagonal), None, 0)
    pair_send(partial, landing, pair_sems, pair_recv, core, diagonal)
    peers = (core, across, diagonal)
    for i, peer in enumerate(peers):
        remote(deg.at[peer], deg_in.at[i], deg_send.at[i], deg_recv.at[i], tile=peer).start()
    first = remote(partial.at[across], landing.at[1], pair_sems.at[1], pair_recv.at[1], tile=core)
    first.wait_recv()
    passing[...] = (partial[across].astype(F32) + landing[1].astype(F32)).astype(BF)
    cross = remote(passing, other, cross_sem, cross_recv, tile=across)
    cross.start()
    hidden = jnp.dot(feat[...], self_weight[...], preferred_element_type=F32)
    second = remote(partial.at[core], landing.at[0], pair_sems.at[0], pair_recv.at[0], tile=core)
    second.wait_recv()
    degree = deg[t]
    for i, peer in enumerate(peers):
        copy = remote(deg.at[peer], deg_in.at[i], deg_send.at[i], deg_recv.at[i], tile=peer)
        copy.wait_recv()
        degree = degree + deg_in[i]
    blocks, _, size = degree.shape
    columns = feat.shape[1]
    scale = 1.0 / jnp.maximum(degree, 1.0)
    pieces = []
    for b in range(blocks):
        turned = jnp.broadcast_to(scale[b, 0:1, :], (size, size)).T
        pieces.append(jnp.concatenate([turned] * (columns // size), axis=1))
    inverse = jnp.concatenate(pieces, axis=0)
    cross.wait_recv()
    summed = partial[t].astype(F32) + landing[0].astype(F32) + other[...].astype(F32)
    mean_rows = (summed * inverse).astype(BF)
    hidden = hidden + jnp.dot(mean_rows, neigh_weight[...], preferred_element_type=F32)
    sig = jax.nn.sigmoid(hidden)
    grads = (grad_out[...].astype(F32) * sig * (1.0 + hidden * (1.0 - sig))).astype(BF)
    back = lax.dot_general(grads, neigh_weight[...], NT, preferred_element_type=F32)
    mine_b[...] = (back * inverse).astype(BF)
    tile_gather_start(mine_b, grad_all, t, core, across, tile_send, tile_recv)
    grad_all[t] = mine_b[...]
    activated[...] = (hidden * sig).astype(BF)
    grad_hidden[...] = grads
    self_term[...] = lax.dot_general(feat[...], grads, TN, preferred_element_type=F32)
    tile_gather_middle(grad_all, core, across, tile_send, tile_recv)
    neigh_term[...] = lax.dot_general(mean_rows, grads, TN, preferred_element_type=F32)
    tile_gather_end(mine_b, grad_all, core, across, diagonal, tile_send, tile_recv)
    first.wait_send()
    second.wait_send()
    cross.wait_send()
    for i, peer in enumerate(peers):
        remote(deg.at[peer], deg_in.at[i], deg_send.at[i], deg_recv.at[i], tile=peer).wait_send()


def return_kernel(
    domains,
    local,
    halo,
    hub,
    halo_ids,
    hub_ids,
    grad_hidden,
    self_weight,
    out,
    landing,
    other,
    passing,
    halo_in,
    hub_in,
    halo_pass,
    hub_pass,
    halo_other,
    hub_other,
    halo_total,
    hub_total,
    halo_back,
    hub_back,
    acc,
    pair_sems,
    pair_recv,
    cross_sem,
    cross_recv,
    halo_send,
    hub_send,
    halo_recv,
    hub_recv,
    halo_csend,
    hub_csend,
    halo_crecv,
    hub_crecv,
    halo_dsend,
    hub_dsend,
    halo_drecv,
    hub_drecv,
    halo_core,
    halo_across,
    hub_core,
    hub_across,
):
    count = domains // 4
    me, t, core, across, diagonal, slots = places(domains)
    mine, theirs = slots(t), slots(across)
    quarter = out.shape[0]
    greet(me, (core, across, diagonal), mine, count)
    both = (
        (halo, halo_in, halo_send, halo_recv, halo_pass, halo_other, halo_csend, halo_crecv, halo_total),
        (hub, hub_in, hub_send, hub_recv, hub_pass, hub_other, hub_csend, hub_crecv, hub_total),
    )

    def start_for(who):
        spots = slots(who)

        def body(i):
            s = spots(i)
            for part, landed, send, recv, *_ in both:
                remote(part.at[s], landed.at[s], send.at[s], recv.at[s], tile=core).start()

        each(count, body)

    start_for(diagonal)
    start_for(core)
    pair_send(local, landing, pair_sems, pair_recv, core, diagonal)

    def pass_on(i):
        s = theirs(i)
        for part, landed, send, recv, passed, crossed, csend, crecv, total in both:
            remote(part.at[s], landed.at[s], send.at[s], recv.at[s], tile=core).wait_recv()
            passed[i] = (part[s].astype(F32) + landed[s].astype(F32)).astype(BF)
            remote(passed.at[i], crossed.at[i], csend.at[i], crecv.at[i], tile=across).start()

    each(count, pass_on)
    first = remote(local.at[across], landing.at[1], pair_sems.at[1], pair_recv.at[1], tile=core)
    first.wait_recv()
    passing[...] = (local[across].astype(F32) + landing[1].astype(F32)).astype(BF)
    cross = remote(passing, other, cross_sem, cross_recv, tile=across)

    def own(i):
        s = mine(i)
        for part, landed, send, recv, passed, crossed, csend, crecv, total in both:
            remote(part.at[s], landed.at[s], send.at[s], recv.at[s], tile=core).wait_recv()
            remote(passed.at[i], crossed.at[i], csend.at[i], crecv.at[i], tile=across).wait_recv()
            total[i] = (part[s].astype(F32) + landed[s].astype(F32) + crossed[i].astype(F32)).astype(BF)

    each(count, own)
    pairs = (
        (halo_total, halo_back, halo_dsend, halo_drecv),
        (hub_total, hub_back, hub_dsend, hub_drecv),
    )
    forward = ((halo_core, halo_across), (hub_core, hub_across))
    dom_send(count, me, mine, pairs)
    cross.start()
    acc[...] = lax.dot_general(grad_hidden[...], self_weight[...], NT, preferred_element_type=F32)
    second = remote(local.at[core], landing.at[0], pair_sems.at[0], pair_recv.at[0], tile=core)
    second.wait_recv()
    acc[...] += local[t].astype(F32) + landing[0].astype(F32)
    dom_gather(count, me, t, core, across, diagonal, slots, pairs, forward)

    def pick(ids):
        spot = lax.broadcasted_iota(jnp.int32, (quarter, ids.shape[1]), 0) + t * quarter
        return (spot == ids).astype(F32).astype(BF)

    hub_pick = pick(hub_ids[...])

    def spread(p, carry):
        acc[...] += jnp.dot(pick(halo_ids[p]), halo_back[p], preferred_element_type=F32) + jnp.dot(
            hub_pick, hub_back[p], preferred_element_type=F32
        )
        return carry

    lax.fori_loop(0, domains, spread, 0)
    cross.wait_recv()
    out[...] = (acc[...] + other[...].astype(F32)).astype(BF)
    first.wait_send()
    second.wait_send()
    cross.wait_send()

    def finish(i):
        for part, landed, send, recv, passed, crossed, csend, crecv, total in both:
            for who in (core, diagonal):
                s = slots(who)(i)
                remote(part.at[s], landed.at[s], send.at[s], recv.at[s], tile=core).wait_send()
            remote(passed.at[i], crossed.at[i], csend.at[i], crecv.at[i], tile=across).wait_send()

    each(count, finish)


def on_device(
    features,
    grad_out,
    self_weight,
    neigh_weight,
    edge_tiles,
    tile_dst,
    tile_src,
    halo_send,
    hub_ids,
):
    domains = lax.axis_size("dom")
    groups = lax.axis_size("tile")
    quarter, columns = features.shape
    size = edge_tiles.shape[1]
    vertices = quarter * groups
    halo_total = halo_send.shape[1]
    per_peer = halo_total // domains
    hub_own = hub_ids.shape[0]
    hubs = hub_own * domains
    count = domains // groups
    outs = grad_out.shape[1]
    nl, nh, nb = vertices // size, halo_total // size, hubs // size
    halo_ids = halo_send.reshape(domains, 1, per_peer)
    hub_row = hub_ids.reshape(1, hub_own)
    sem = lambda n: pltpu.SemaphoreType.DMA((n,))
    shape = jax.ShapeDtypeStruct

    def params(number):
        return pltpu.CompilerParams(
            collective_id=number, has_side_effects=True, vmem_limit_bytes=LIMIT
        )

    local, halo, hub = pl.pallas_call(
        functools.partial(collect_kernel, domains),
        out_shape=(
            shape((groups, quarter, columns), BF),
            shape((domains, per_peer, columns), BF),
            shape((domains, hub_own, columns), BF),
        ),
        in_specs=[VMEM] * 3,
        out_specs=(VMEM,) * 3,
        scratch_shapes=[
            pltpu.VMEM((count, per_peer, columns), BF),
            pltpu.VMEM((count, hub_own, columns), BF),
            sem(3),
            sem(4),
            sem(count),
            sem(count),
        ]
        + [sem(domains)] * 6,
        compiler_params=params(0),
        name="collect",
    )(features, halo_ids, hub_row)

    partial, degree = pl.pallas_call(
        forward_kernel,
        out_shape=(shape((nl, size, columns), BF), shape((nl, 8, size), F32)),
        in_specs=[VMEM, SMEM, SMEM, ANY, ANY, ANY],
        out_specs=(VMEM, VMEM),
        scratch_shapes=[
            pltpu.VMEM((nl + nh + nb, size, columns), BF),
            pltpu.VMEM((nl, size, columns), F32),
            sem(3),
        ],
        compiler_params=pltpu.CompilerParams(vmem_limit_bytes=LIMIT),
        name="aggregate",
    )(
        edge_tiles,
        tile_dst,
        tile_src,
        local.reshape(nl, size, columns),
        halo.reshape(nh, size, columns),
        hub.reshape(nb, size, columns),
    )

    block = pltpu.VMEM((quarter, columns), BF)
    activated, grad_hidden, grad_all, self_term, neigh_term = pl.pallas_call(
        functools.partial(dense_kernel, domains),
        out_shape=(
            shape((quarter, outs), BF),
            shape((quarter, outs), BF),
            shape((groups, quarter, columns), BF),
            shape((columns, outs), F32),
            shape((columns, outs), F32),
        ),
        in_specs=[VMEM] * 6,
        out_specs=(VMEM,) * 5,
        scratch_shapes=[
            pltpu.VMEM((2, quarter, columns), BF),
            block,
            block,
            pltpu.VMEM((3, nl // groups, 8, size), F32),
            block,
            sem(2),
            sem(2),
            pltpu.SemaphoreType.DMA,
            pltpu.SemaphoreType.DMA,
            sem(3),
            sem(3),
            sem(3),
            sem(4),
        ],
        compiler_params=params(1),
        name="dense",
    )(
        partial.reshape(groups, quarter, columns),
        degree.reshape(groups, nl // groups, 8, size),
        features,
        grad_out,
        self_weight,
        neigh_weight,
    )

    inv_root = 1.0 / (vertices * domains) ** 0.5
    grad_self, grad_neigh = lax.psum((self_term, neigh_term), ("dom", "tile"))

    back_local, back_halo, back_hub = pl.pallas_call(
        backward_kernel,
        out_shape=(
            shape((nl, size, columns), BF),
            shape((nh, size, columns), BF),
            shape((nb, size, columns), BF),
        ),
        in_specs=[VMEM, SMEM, SMEM, VMEM],
        out_specs=(VMEM,) * 3,
        scratch_shapes=[pltpu.VMEM((nl + nh + nb, size, columns), F32)],
        compiler_params=pltpu.CompilerParams(vmem_limit_bytes=LIMIT),
        name="backward",
    )(edge_tiles, tile_dst, tile_src, grad_all.reshape(nl, size, columns))

    grad_features = pl.pallas_call(
        functools.partial(return_kernel, domains),
        out_shape=shape((quarter, columns), BF),
        in_specs=[VMEM] * 7,
        out_specs=VMEM,
        scratch_shapes=[
            pltpu.VMEM((2, quarter, columns), BF),
            block,
            block,
            pltpu.VMEM((domains, per_peer, columns), BF),
            pltpu.VMEM((domains, hub_own, columns), BF),
            pltpu.VMEM((count, per_peer, columns), BF),
            pltpu.VMEM((count, hub_own, columns), BF),
            pltpu.VMEM((count, per_peer, columns), BF),
            pltpu.VMEM((count, hub_own, columns), BF),
            pltpu.VMEM((count, per_peer, columns), BF),
            pltpu.VMEM((count, hub_own, columns), BF),
            pltpu.VMEM((domains, per_peer, columns), BF),
            pltpu.VMEM((domains, hub_own, columns), BF),
            pltpu.VMEM((quarter, columns), F32),
            sem(2),
            sem(2),
            pltpu.SemaphoreType.DMA,
            pltpu.SemaphoreType.DMA,
        ]
        + [sem(domains)] * 4
        + [sem(count)] * 4
        + [sem(count)] * 2
        + [sem(domains)] * 2
        + [sem(domains)] * 4,
        compiler_params=params(2),
        name="give_back",
    )(
        back_local.reshape(groups, quarter, columns),
        back_halo.reshape(domains, per_peer, columns),
        back_hub.reshape(domains, hub_own, columns),
        halo_ids,
        hub_row,
        grad_hidden,
        self_weight,
    )
    return activated, grad_features, grad_self * inv_root, grad_neigh * inv_root


def solution(mesh):
    return jax.shard_map(
        on_device,
        mesh=mesh,
        in_specs=(
            P(("dom", "tile"), None),
            P(("dom", "tile"), None),
            P(),
            P(),
            P(("dom", "tile"), None, None),
            P(("dom", "tile")),
            P(("dom", "tile")),
            P("dom", None),
            P("dom"),
        ),
        out_specs=(P(("dom", "tile"), None), P(("dom", "tile"), None), P(), P()),
        check_vma=False,
    )
```

time: 455 us -> 206 us (0.45)
  waiting for transfers between devices: 289 us -> 99.8 us
  Pallas kernels: 0 us -> 80.4 us
  blocking collectives: 42.8 us -> 0 us
  matrix products: 37.7 us -> 0 us
  local copies, waits for them, and re-layouts: 45.4 us -> 9.5 us
  starting transfers between devices: 11.6 us -> 0.04 us
  other arithmetic: 12.7 us -> 1.85 us
    reduce_scatter x3 -> x0, waiting for transfers between devices: 92.3 us -> none  [the longest x1 54.6 us: on_device(): lax.psum_scatter(hub_grad, 'dom', scatter_dimension=0, tiled=True)]
    pallas_call x0 -> x5, Pallas kernels: none -> 80.4 us  [the longest x1 25.7 us: on_device(): pl.pallas_call(functools.partial(collect_kernel, domains), out_shape=(sha...]
    psum x2 -> x1, waiting for transfers between devices: 159 us -> 99.8 us  [on_device(): grad_self, grad_neigh = lax.psum((self_term, neigh_term), ('dom', 'tile'))]
    dot_general x11 -> x0, matrix products: 37.7 us -> none  [the longest x1 8.19 us: on_device(): jnp.einsum('tij,tjf->tif', edge_tiles, picked, preferred_element_type=jnp...]
    all_gather x2 -> x0, waiting for transfers between devices: 37 us -> none  [the longest x1 20.4 us: on_device(): whole_rows = lax.all_gather(features, 'tile', axis=0, tiled=True)]
    all_gather x1 -> x0, blocking collectives: 36.8 us -> none  [on_device(): hub_rows = lax.all_gather(own_hubs, 'dom', axis=0, tiled=True)]
    dot_general x2 -> x0, local copies, waits for them, and re-layouts: 19.3 us -> none  [the longest x1 9.64 us: on_device(): jnp.einsum('tij,tjf->tif', edge_tiles, picked, preferred_element_type=jnp...]
    gather x4 -> x0, local copies, waits for them, and re-layouts: 19.1 us -> none  [the longest x1 6.81 us: on_device(): dst_pick = grad_whole.reshape(dst_blocks, tile_size, columns)[tile_dst]]
  transfers between devices with their start and end apart: 9 -> 1, of which waited for: 7 -> 1; matrix products, arithmetic and copies ran while one was open for 4% -> 0% of each run, Pallas kernels for 0% -> 15%
where the time goes in v1:
time: 206 us
  waiting for transfers between devices  99.8 us (48%)
  Pallas kernels  80.4 us (39%)
  between operations  14.2 us (7%)
  local copies, waits for them, and re-layouts  9.5 us (5%)
    psum x1, waiting for transfers between devices, on_device(): grad_self, grad_neigh = lax.psum((self_term, neigh_term), ('dom', 'tile'))  99.8 us
    pallas_call x1, Pallas kernels, on_device(): pl.pallas_call(functools.partial(collect_kernel, domains), out_shape=(sha...  25.7 us
    pallas_call x1, Pallas kernels, on_device(): pl.pallas_call(functools.partial(return_kernel, domains), out_shape=shape...  24.2 us
    pallas_call x1, Pallas kernels, on_device(): pl.pallas_call(functools.partial(dense_kernel, domains), out_shape=(shape...  18.7 us
    unnamed x42, local copies, waits for them, and re-layouts  9.5 us
    pallas_call x1, Pallas kernels, on_device(): pl.pallas_call(forward_kernel, out_shape=(shape((nl, size, columns), BF),...  6.05 us
    pallas_call x1, Pallas kernels, on_device(): pl.pallas_call(backward_kernel, out_shape=(shape((nl, size, columns), BF)...  5.7 us
  transfers between devices with their start and end apart: 1, of which 1 were waited for; matrix products, arithmetic and copies ran while one was open for 0% of the time, Pallas kernels for 15%

profile of v1, /device:TPU:0, one launch (start us, length us, event | category | flops | bytes accessed | tf_op | source)
XLA Modules:
  0.0 205.7 jit_solution(9519126564473781242)
XLA Ops:
  7.2 0.0 all-reduce.3.cloned.1.call-start
  7.2 0.9 copy-done.2
  8.2 0.7 copy-done.12
  8.9 0.7 copy-done.18
  9.5 25.7 %collect.1 = (bf16[4,512,256]{2,1,0:T(8,128)(2,1)S(1)}, bf16[8,128,256]{2,1,0:T(8,128)(2,1)S(1)}, bf16[8,32,256]{2,1,0:T(8,128)(2,1)S(1)}) custom-call(bf16[512,256]{1,0:T(8,128)(2,1)S(1)} %copy-done.2, s32[8,1,128]{2,1,0:T(1,128)S(1)} %bitcast.16, s32[1,32]{1,0:T(1,128)S(1)} %bitcast.18), custom_call_target="tpu_custom_call" | custom-call | tf_op jit(solution)/shard_map/collect/pallas_call | solution.py:516
  35.2 1.7 copy-done
  36.9 0.7 copy-done.14
  37.5 0.7 copy-done.16
  38.2 6.1 %aggregate.1 = (bf16[16,128,256]{2,1,0:T(8,128)(2,1)S(1)}, f32[16,8,128]{2,1,0:T(8,128)S(1)}) custom-call(bf16[72,128,128]{2,1,0:T(8,128)(2,1)S(1)} %copy-done, s32[72]{0:T(128)S(1)} %copy-done.14, s32[72]{0:T(128)S(1)} %copy-done.16, bf16[16,128,256]{2,1,0:T(8,128)(2,1)S(1)} %bitcast.9, bf16[8,128,256]{2,1,0:T(8,128)(2,1)S(1)} %get-tuple-element.18.halo, ...), custom_call_target="tpu_custom_call" | custom-call | tf_op jit(solution)/shard_map/aggregate/pallas_call | solution.py:538
  44.3 18.7 %dense.1 = (bf16[512,256]{1,0:T(8,128)(2,1)S(1)}, bf16[512,256]{1,0:T(8,128)(2,1)S(1)}, bf16[4,512,256]{2,1,0:T(8,128)(2,1)S(1)}, f32[256,256]{1,0:T(8,128)S(1)}, f32[256,256]{1,0:T(8,128)S(1)}) custom-call(bf16[4,512,256]{2,1,0:T(8,128)(2,1)S(1)} %bitcast.11, f32[4,4,8,128]{3,2,1,0:T(8,128)S(1)} %bitcast.15, bf16[512,256]{1,0:T(8,128)(2,1)S(1)} %copy-done.2, ...), custom_call_target="tpu_custom_call" | custom-call | tf_op jit(solution)/shard_map/dense/pallas_call | solution.py:560
  63.0 0.0 copy-start.4
  63.0 0.7 copy-done.4
  63.7 0.7 copy-done.6
  64.4 0.7 copy-done.7
  65.1 0.7 copy-done.9
  65.8 0.0 all-reduce.3.cloned.1.call-update
  65.8 0.0 copy-start.10
  65.9 5.7 %backward.1 = (bf16[16,128,256]{2,1,0:T(8,128)(2,1)S(1)}, bf16[8,128,256]{2,1,0:T(8,128)(2,1)S(1)}, bf16[2,128,256]{2,1,0:T(8,128)(2,1)S(1)}) custom-call(bf16[72,128,128]{2,1,0:T(8,128)(2,1)S(1)} %copy-done.1, s32[72]{0:T(128)S(1)} %copy-done.15, s32[72]{0:T(128)S(1)} %copy-done.17, bf16[16,128,256]{2,1,0:T(8,128)(2,1)S(1)} %bitcast.10), custom_call_target="tpu_custom_call" | custom-call | tf_op jit(solution)/shard_map/backward/pallas_call | solution.py:600
  71.6 0.0 copy-start.5
  71.6 24.2 %give_back.1 = bf16[512,256]{1,0:T(8,128)(2,1)S(1)} custom-call(bf16[4,512,256]{2,1,0:T(8,128)(2,1)S(1)} %bitcast.12, bf16[8,128,256]{2,1,0:T(8,128)(2,1)S(1)} %get-tuple-element.25.halo, bf16[8,32,256]{2,1,0:T(8,128)(2,1)S(1)} %bitcast.14, s32[8,1,128]{2,1,0:T(1,128)S(1)} %bitcast.17, s32[1,32]{1,0:T(1,128)S(1)} %bitcast.19, ...), custom_call_target="tpu_custom_call" | custom-call | tf_op jit(solution)/shard_map/give_back/pallas_call | solution.py:614
  95.9 99.8 %all-reduce.3.cloned.1.call-done = (f32[256,256]{1,0:T(8,128)}, f32[256,256]{1,0:T(8,128)}) async-done(((f32[256,256]{1,0:T(8,128)}, f32[256,256]{1,0:T(8,128)}), (f32[256,256]{1,0:T(8,128)}, f32[256,256]{1,0:T(8,128)})) %all-reduce.3.cloned.1.call-update) | async-done | bytes 524304 | tf_op jit(solution)/shard_map/psum | solution.py:598
  195.6 1.9 broadcast_multiply_fusion
  197.5 0.7 copy.17
  198.2 0.7 copy.18
  (27 shorter events, 0.1 us)
Async XLA Ops:
  7.2 188.5 %all-reduce.3.cloned.1.call-start = ((), (), s32[]{:S(2)}) async-start(), calls=%async_computation | async-start | bytes 1048576 | tf_op jit(solution)/shard_map/psum | solution.py:598
  7.2 1.0 copy-start.2
  8.2 0.7 copy-start.12
  8.8 0.7 copy-start.18
  9.5 34.7 %copy-start.3 = (bf16[256,256]{1,0:T(8,128)(2,1)S(1)}, bf16[256,256]{1,0:T(8,128)(2,1)}, u32[]{:S(2)}) copy-start(bf16[256,256]{1,0:T(8,128)(2,1)} %self_weight.3) | copy-start | bytes 393220
  9.5 34.8 %copy-start.11 = (bf16[256,256]{1,0:T(8,128)(2,1)S(1)}, bf16[256,256]{1,0:T(8,128)(2,1)}, u32[]{:S(2)}) copy-start(bf16[256,256]{1,0:T(8,128)(2,1)} %neigh_weight.1) | copy-start | bytes 393220
  35.2 1.7 copy-start
  36.9 0.7 copy-start.14
  37.5 0.7 copy-start.16
  38.2 6.1 %copy-start.8 = (bf16[512,256]{1,0:T(8,128)(2,1)S(1)}, bf16[512,256]{1,0:T(8,128)(2,1)}, u32[]{:S(2)}) copy-start(bf16[512,256]{1,0:T(8,128)(2,1)} %grad_out.1) | copy-start | bytes 786436
  38.2 27.6 %copy-start.1 = (bf16[72,128,128]{2,1,0:T(8,128)(2,1)S(1)}, bf16[72,128,128]{2,1,0:T(8,128)(2,1)}, u32[]{:S(2)}) copy-start(bf16[72,128,128]{2,1,0:T(8,128)(2,1)} %tiles.3) | copy-start | bytes 7077892
  38.2 27.7 %copy-start.15 = (s32[72]{0:T(128)S(1)}, s32[72]{0:T(128)}, u32[]{:S(2)}) copy-start(s32[72]{0:T(128)} %dst.3) | copy-start | bytes 868
  38.2 27.7 %copy-start.17 = (s32[72]{0:T(128)S(1)}, s32[72]{0:T(128)}, u32[]{:S(2)}) copy-start(s32[72]{0:T(128)} %src.3) | copy-start | bytes 868
  63.0 0.7 copy-start.4
  63.7 0.7 copy-start.6
  64.4 0.7 copy-start.7
  65.1 0.7 copy-start.9
  65.8 5.8 %copy-start.13 = (s32[1,1024]{1,0:T(1,128)S(1)}, s32[1,1024]{1,0:T(1,128)}, u32[]{:S(2)}) copy-start(s32[1,1024]{1,0:T(1,128)} %param.16) | copy-start | bytes 12292
  65.8 5.8 %copy-start.19 = (s32[32]{0:T(128)S(1)}, s32[32]{0:T(128)}, u32[]{:S(2)}) copy-start(s32[32]{0:T(128)} %param.17) | copy-start | bytes 388
  65.8 5.8 %copy-start.10 = (bf16[512,256]{1,0:T(8,128)(2,1)S(1)}, bf16[512,256]{1,0:T(8,128)(2,1)}, u32[]{:S(2)}) copy-start(bf16[512,256]{1,0:T(8,128)(2,1)} %copy-done.9) | copy-start | bytes 786436
  71.6 125.9 %copy-start.5 = (bf16[512,256]{1,0:T(8,128)(2,1)S(1)}, bf16[512,256]{1,0:T(8,128)(2,1)}, u32[]{:S(2)}) copy-start(bf16[512,256]{1,0:T(8,128)(2,1)} %copy-done.4) | copy-start | bytes 786436
Sparse Core Ops, SparseCore 0:
  65.9 129.6 all-reduce.2

commit v2 on v1

--- a/solution.py
+++ b/solution.py
@@ -13,7 +13,7 @@
 VMEM = pl.BlockSpec(memory_space=pltpu.VMEM)
 SMEM = pl.BlockSpec(memory_space=pltpu.SMEM)
 ANY = pl.BlockSpec(memory_space=pl.ANY)
-LIMIT = 40 * 1024 * 1024
+LIMIT = 20 * 1024 * 1024
 NT = (((1,), (1,)), ((), ()))
 TN = (((0,), (0,)), ((), ()))
 
@@ -43,7 +43,7 @@
     )
 
 
-def greet(me, peers, others, count):
+def greet(me, peers, others, count, own):
     barrier = pltpu.get_barrier_semaphore()
     for peer in peers:
         pl.semaphore_signal(barrier, inc=1, device_id={"tile": peer}, device_id_type=MESH)
@@ -54,8 +54,11 @@
         def _():
             pl.semaphore_signal(barrier, inc=1, device_id={"dom": there}, device_id_type=MESH)
 
-    own = jnp.where(lax.rem(others(0) + 4 * count - me, 4) == 0, 1, 0) if count else 0
     pl.semaphore_wait(barrier, len(peers) + count - own)
+
+
+def met(me, mine, domains):
+    return jnp.where(lax.rem(mine(0) + 4 * domains - me, 4) == 0, 1, 0)
 
 
 def each(count, body):
@@ -146,6 +149,10 @@
 def tile_gather_end(src, out, core, across, diagonal, send, recv):
     for who in (core, diagonal):
         remote(out.at[who], out.at[who], send.at[1], recv.at[who], tile=core).wait_recv()
+    tile_gather_sent(src, out, core, across, send, recv)
+
+
+def tile_gather_sent(src, out, core, across, send, recv):
     remote(src, out.at[core], send.at[0], recv.at[core], tile=across).wait_send()
     remote(src, out.at[core], send.at[1], recv.at[core], tile=core).wait_send()
     remote(out.at[across], out.at[across], send.at[2], recv.at[core], tile=core).wait_send()
@@ -161,6 +168,8 @@
     hub,
     staged_halo,
     staged_hub,
+    halo_acc,
+    hub_acc,
     tile_send,
     tile_recv,
     halo_send,
@@ -176,32 +185,45 @@
     me, t, core, across, diagonal, slots = places(domains)
     mine = slots(t)
     quarter = feat.shape[0]
-    greet(me, (core, across, diagonal), mine, count)
+    greet(me, (core, across, diagonal), mine, count, met(me, mine, domains))
     tile_gather_start(feat, local, t, core, across, tile_send, tile_recv)
     local[t] = feat[...]
-    tile_gather_middle(local, core, across, tile_send, tile_recv)
-    tile_gather_end(feat, local, core, across, diagonal, tile_send, tile_recv)
-
-    def rows(ids):
-        total = None
-        for part in range(4):
+
+    def add(part, source, first):
+        values = source[...]
+
+        def term(ids):
             spot = lax.broadcasted_iota(jnp.int32, (quarter, ids.shape[1]), 0) + part * quarter
             chosen = (spot == ids).astype(F32).astype(BF)
-            term = lax.dot_general(chosen, local[part], TN, preferred_element_type=F32)
-            total = term if total is None else total + term
-        return total.astype(BF)
-
-    own_hubs = rows(hub_ids[...])
+            return lax.dot_general(chosen, values, TN, preferred_element_type=F32)
+
+        def body(i):
+            found = term(halo_ids[mine(i)])
+            halo_acc[i] = found if first else halo_acc[i] + found
+
+        each(count, body)
+        found = term(hub_ids[...])
+        hub_acc[...] = found if first else hub_acc[...] + found
+
+    add(t, feat, True)
+    remote(feat, local.at[core], tile_send.at[1], tile_recv.at[core], tile=core).wait_recv()
+    add(core, local.at[core], False)
+    tile_gather_middle(local, core, across, tile_send, tile_recv)
+    add(across, local.at[across], False)
+    remote(feat, local.at[diagonal], tile_send.at[2], tile_recv.at[diagonal], tile=core).wait_recv()
+    add(diagonal, local.at[diagonal], False)
+    own_hubs = hub_acc[...].astype(BF)
 
     def body(i):
         staged_hub[i] = own_hubs
-        staged_halo[i] = rows(halo_ids[mine(i)])
+        staged_halo[i] = halo_acc[i].astype(BF)
 
     each(count, body)
     pairs = ((staged_halo, halo, halo_send, halo_recv), (staged_hub, hub, hub_send, hub_recv))
     forward = ((halo_core, halo_across), (hub_core, hub_across))
     dom_send(count, me, mine, pairs)
     dom_gather(count, me, t, core, across, diagonal, slots, pairs, forward)
+    tile_gather_sent(feat, local, core, across, tile_send, tile_recv)
 
 
 def forward_kernel(tiles, dst, src, local, halo, hub, out, deg, source, acc, sems):
@@ -241,7 +263,9 @@
     out[...] = acc[...].astype(BF)
 
 
-def backward_kernel(tiles, dst, src, grad, local, halo, hub, acc):
+def backward_kernel(tiles, dst, src, grad, active, local, halo, hub, active_out, acc, done):
+    passing = pltpu.make_async_copy(active, active_out, done)
+    passing.start()
     nl, nh = local.shape[0], halo.shape[0]
     acc[...] = jnp.zeros_like(acc)
     step = 4
@@ -264,6 +288,7 @@
     local[...] = acc[pl.ds(0, nl)].astype(BF)
     halo[...] = acc[pl.ds(nl, nh)].astype(BF)
     hub[...] = acc[pl.ds(nl + nh, hub.shape[0])].astype(BF)
+    passing.wait()
 
 
 def pair_send(partial, landing, send, recv, core, diagonal):
@@ -282,13 +307,13 @@
     activated,
     grad_hidden,
     grad_all,
-    self_term,
-    neigh_term,
+    terms,
     landing,
     other,
     passing,
     deg_in,
     mine_b,
+    means,
     pair_sems,
     pair_recv,
     cross_sem,
@@ -299,17 +324,22 @@
     tile_recv,
 ):
     me, t, core, across, diagonal, slots = places(domains)
-    greet(me, (core, across, diagonal), None, 0)
+    chunks, rows = passing.shape[0], passing.shape[1]
+    greet(me, (core, across, diagonal), None, 0, 0)
     pair_send(partial, landing, pair_sems, pair_recv, core, diagonal)
     peers = (core, across, diagonal)
     for i, peer in enumerate(peers):
         remote(deg.at[peer], deg_in.at[i], deg_send.at[i], deg_recv.at[i], tile=peer).start()
     first = remote(partial.at[across], landing.at[1], pair_sems.at[1], pair_recv.at[1], tile=core)
     first.wait_recv()
-    passing[...] = (partial[across].astype(F32) + landing[1].astype(F32)).astype(BF)
-    cross = remote(passing, other, cross_sem, cross_recv, tile=across)
-    cross.start()
-    hidden = jnp.dot(feat[...], self_weight[...], preferred_element_type=F32)
+    crosses = []
+    for c in range(chunks):
+        span = pl.ds(c * rows, rows)
+        passing[c] = (partial[across, span].astype(F32) + landing[1, span].astype(F32)).astype(BF)
+        cross = remote(passing.at[c], other.at[c], cross_sem.at[c], cross_recv.at[c], tile=across)
+        cross.start()
+        crosses.append(cross)
+    hidden_self = jnp.dot(feat[...], self_weight[...], preferred_element_type=F32)
     second = remote(partial.at[core], landing.at[0], pair_sems.at[0], pair_recv.at[0], tile=core)
     second.wait_recv()
     degree = deg[t]
@@ -324,32 +354,54 @@
     for b in range(blocks):
         turned = jnp.broadcast_to(scale[b, 0:1, :], (size, size)).T
         pieces.append(jnp.concatenate([turned] * (columns // size), axis=1))
-    inverse = jnp.concatenate(pieces, axis=0)
-    cross.wait_recv()
-    summed = partial[t].astype(F32) + landing[0].astype(F32) + other[...].astype(F32)
-    mean_rows = (summed * inverse).astype(BF)
-    hidden = hidden + jnp.dot(mean_rows, neigh_weight[...], preferred_element_type=F32)
-    sig = jax.nn.sigmoid(hidden)
-    grads = (grad_out[...].astype(F32) * sig * (1.0 + hidden * (1.0 - sig))).astype(BF)
-    back = lax.dot_general(grads, neigh_weight[...], NT, preferred_element_type=F32)
-    mine_b[...] = (back * inverse).astype(BF)
-    tile_gather_start(mine_b, grad_all, t, core, across, tile_send, tile_recv)
-    grad_all[t] = mine_b[...]
-    activated[...] = (hidden * sig).astype(BF)
-    grad_hidden[...] = grads
-    self_term[...] = lax.dot_general(feat[...], grads, TN, preferred_element_type=F32)
-    tile_gather_middle(grad_all, core, across, tile_send, tile_recv)
-    neigh_term[...] = lax.dot_general(mean_rows, grads, TN, preferred_element_type=F32)
-    tile_gather_end(mine_b, grad_all, core, across, diagonal, tile_send, tile_recv)
+    inverse_all = jnp.concatenate(pieces, axis=0)
+    for c in range(chunks):
+        span = pl.ds(c * rows, rows)
+        inverse = inverse_all[c * rows : (c + 1) * rows]
+        summed = partial[t, span].astype(F32) + landing[0, span].astype(F32)
+        crosses[c].wait_recv()
+        summed = summed + other[c].astype(F32)
+        mean_rows = (summed * inverse).astype(BF)
+        means[span] = mean_rows
+        hidden = hidden_self[c * rows : (c + 1) * rows] + jnp.dot(
+            mean_rows, neigh_weight[...], preferred_element_type=F32
+        )
+        sig = jax.nn.sigmoid(hidden)
+        grads = (grad_out[span].astype(F32) * sig * (1.0 + hidden * (1.0 - sig))).astype(BF)
+        back = lax.dot_general(grads, neigh_weight[...], NT, preferred_element_type=F32)
+        mine_b[c] = (back * inverse).astype(BF)
+        landed = grad_all.at[:, c]
+        tile_gather_start(mine_b.at[c], landed, t, core, across, tile_send.at[c], tile_recv.at[c])
+        grad_all[t, c] = mine_b[c]
+        activated[span] = (hidden * sig).astype(BF)
+        grad_hidden[span] = grads
+    quarter = terms.shape[1]
+
+    def term(values, place):
+        found = lax.dot_general(values, grad_hidden[...], TN, preferred_element_type=F32)
+        terms[place] = found[:quarter].astype(BF)
+        terms[place + 1] = found[quarter:].astype(BF)
+
+    term(feat[...], 0)
+    for c in range(chunks):
+        tile_gather_middle(grad_all.at[:, c], core, across, tile_send.at[c], tile_recv.at[c])
+    term(means[...], 2)
+    for c in range(chunks):
+        tile_gather_end(
+            mine_b.at[c], grad_all.at[:, c], core, across, diagonal, tile_send.at[c], tile_recv.at[c]
+        )
     first.wait_send()
     second.wait_send()
-    cross.wait_send()
+    for cross in crosses:
+        cross.wait_send()
     for i, peer in enumerate(peers):
         remote(deg.at[peer], deg_in.at[i], deg_send.at[i], deg_recv.at[i], tile=peer).wait_send()
 
 
 def return_kernel(
     domains,
+    inside,
+    inv_root,
     local,
     halo,
     hub,
@@ -357,7 +409,9 @@
     hub_ids,
     grad_hidden,
     self_weight,
+    terms,
     out,
+    term_out,
     landing,
     other,
     passing,
@@ -371,6 +425,14 @@
     hub_total,
     halo_back,
     hub_back,
+    term_in,
+    term_pass,
+    term_other,
+    term_cut,
+    term_rs,
+    term_sum,
+    term_ag,
+    term_mine,
     acc,
     pair_sems,
     pair_recv,
@@ -392,12 +454,25 @@
     halo_across,
     hub_core,
     hub_across,
+    term_psend,
+    term_precv,
+    term_csend,
+    term_crecv,
+    term_rsend,
+    term_rrecv,
+    term_asend,
+    term_arecv,
+    term_tsend,
+    term_trecv,
 ):
     count = domains // 4
     me, t, core, across, diagonal, slots = places(domains)
     mine, theirs = slots(t), slots(across)
     quarter = out.shape[0]
-    greet(me, (core, across, diagonal), mine, count)
+    if inside:
+        greet(me, (core, across, diagonal), lambda i: i, domains, 1)
+    else:
+        greet(me, (core, across, diagonal), mine, count, met(me, mine, domains))
     both = (
         (halo, halo_in, halo_send, halo_recv, halo_pass, halo_other, halo_csend, halo_crecv, halo_total),
         (hub, hub_in, hub_send, hub_recv, hub_pass, hub_other, hub_csend, hub_crecv, hub_total),
@@ -415,6 +490,8 @@
 
     start_for(diagonal)
     start_for(core)
+    if inside:
+        pair_send(terms, term_in, term_psend, term_precv, core, diagonal)
     pair_send(local, landing, pair_sems, pair_recv, core, diagonal)
 
     def pass_on(i):
@@ -425,6 +502,19 @@
             remote(passed.at[i], crossed.at[i], csend.at[i], crecv.at[i], tile=across).start()
 
     each(count, pass_on)
+    if inside:
+        term_first = remote(
+            terms.at[across], term_in.at[1], term_psend.at[1], term_precv.at[1], tile=core
+        )
+        term_second = remote(
+            terms.at[core], term_in.at[0], term_psend.at[0], term_precv.at[0], tile=core
+        )
+        term_cross = remote(
+            term_pass, term_other, term_csend.at[0], term_crecv.at[0], tile=across
+        )
+        term_first.wait_recv()
+        term_pass[...] = (terms[across].astype(F32) + term_in[1].astype(F32)).astype(BF)
+        term_cross.start()
     first = remote(local.at[across], landing.at[1], pair_sems.at[1], pair_recv.at[1], tile=core)
     first.wait_recv()
     passing[...] = (local[across].astype(F32) + landing[1].astype(F32)).astype(BF)
@@ -445,11 +535,48 @@
     forward = ((halo_core, halo_across), (hub_core, hub_across))
     dom_send(count, me, mine, pairs)
     cross.start()
+    if inside:
+        term_second.wait_recv()
+        term_cross.wait_recv()
+        cut = terms[t].astype(F32) + term_in[0].astype(F32) + term_other[...].astype(F32)
+        term_cut[...] = cut.reshape(term_cut.shape)
+
+        def to_all(source, landed, send, recv, start):
+            for p in range(domains):
+
+                @pl.when(p != me)
+                def _():
+                    if start:
+                        remote(source(p), landed.at[me], send.at[p], recv.at[me], dom=p).start()
+                    else:
+                        remote(source(p), landed.at[p], send.at[p], recv.at[p], dom=p).wait_recv()
+
+        def all_sent(source, landed, send, recv):
+            for p in range(domains):
+
+                @pl.when(p != me)
+                def _():
+                    remote(source(p), landed.at[p], send.at[p], recv.at[p], dom=p).wait_send()
+
+        scatter = (lambda p: term_cut.at[p], term_rs, term_rsend, term_rrecv)
+        collect = (lambda p: term_sum, term_ag, term_asend, term_arecv)
+        to_all(*scatter, True)
+        term_rs[me] = term_cut[me]
     acc[...] = lax.dot_general(grad_hidden[...], self_weight[...], NT, preferred_element_type=F32)
     second = remote(local.at[core], landing.at[0], pair_sems.at[0], pair_recv.at[0], tile=core)
     second.wait_recv()
     acc[...] += local[t].astype(F32) + landing[0].astype(F32)
+    if inside:
+        to_all(*scatter, False)
+        term_sum[...] = jnp.sum(term_rs[...], axis=0) * inv_root
+        to_all(*collect, True)
+        term_ag[me] = term_sum[...]
     dom_gather(count, me, t, core, across, diagonal, slots, pairs, forward)
+    if inside:
+        to_all(*collect, False)
+        term_mine[...] = term_ag[...].reshape(term_mine.shape)
+        tile_gather_start(term_mine, term_out, t, core, across, term_tsend, term_trecv)
+        term_out[t] = term_mine[...]
 
     def pick(ids):
         spot = lax.broadcasted_iota(jnp.int32, (quarter, ids.shape[1]), 0) + t * quarter
@@ -466,6 +593,16 @@
     lax.fori_loop(0, domains, spread, 0)
     cross.wait_recv()
     out[...] = (acc[...] + other[...].astype(F32)).astype(BF)
+    if inside:
+        tile_gather_middle(term_out, core, across, term_tsend, term_trecv)
+        tile_gather_end(term_mine, term_out, core, across, diagonal, term_tsend, term_trecv)
+        term_first.wait_send()
+        term_second.wait_send()
+        term_cross.wait_send()
+        all_sent(*scatter)
+        all_sent(*collect)
+    else:
+        term_out[...] = terms[...].astype(F32)
     first.wait_send()
     second.wait_send()
     cross.wait_send()
@@ -508,6 +645,10 @@
     sem = lambda n: pltpu.SemaphoreType.DMA((n,))
     shape = jax.ShapeDtypeStruct
 
+    def cost(mib):
+        return pl.CostEstimate(flops=mib << 26, bytes_accessed=mib << 20, transcendentals=0)
+
+
     def params(number):
         return pltpu.CompilerParams(
             collective_id=number, has_side_effects=True, vmem_limit_bytes=LIMIT
@@ -525,6 +666,8 @@
         scratch_shapes=[
             pltpu.VMEM((count, per_peer, columns), BF),
             pltpu.VMEM((count, hub_own, columns), BF),
+            pltpu.VMEM((count, per_peer, columns), F32),
+            pltpu.VMEM((hub_own, columns), F32),
             sem(3),
             sem(4),
             sem(count),
@@ -532,6 +675,7 @@
         ]
         + [sem(domains)] * 6,
         compiler_params=params(0),
+        cost_estimate=cost(30),
         name="collect",
     )(features, halo_ids, hub_row)
 
@@ -546,6 +690,7 @@
             sem(3),
         ],
         compiler_params=pltpu.CompilerParams(vmem_limit_bytes=LIMIT),
+        cost_estimate=cost(12),
         name="aggregate",
     )(
         edge_tiles,
@@ -556,34 +701,38 @@
         hub.reshape(nb, size, columns),
     )
 
+    chunks = 2
     block = pltpu.VMEM((quarter, columns), BF)
-    activated, grad_hidden, grad_all, self_term, neigh_term = pl.pallas_call(
+    part = pltpu.VMEM((chunks, quarter // chunks, columns), BF)
+    term_rows = 2 * columns // groups
+    activated, grad_hidden, grad_all, terms = pl.pallas_call(
         functools.partial(dense_kernel, domains),
         out_shape=(
             shape((quarter, outs), BF),
             shape((quarter, outs), BF),
-            shape((groups, quarter, columns), BF),
-            shape((columns, outs), F32),
-            shape((columns, outs), F32),
+            shape((groups, chunks, quarter // chunks, columns), BF),
+            shape((groups, term_rows, outs), BF),
         ),
         in_specs=[VMEM] * 6,
-        out_specs=(VMEM,) * 5,
+        out_specs=(VMEM,) * 4,
         scratch_shapes=[
             pltpu.VMEM((2, quarter, columns), BF),
-            block,
-            block,
+            part,
+            part,
             pltpu.VMEM((3, nl // groups, 8, size), F32),
+            part,
             block,
             sem(2),
             sem(2),
-            pltpu.SemaphoreType.DMA,
-            pltpu.SemaphoreType.DMA,
+            sem(chunks),
+            sem(chunks),
             sem(3),
             sem(3),
-            sem(3),
-            sem(4),
+            pltpu.SemaphoreType.DMA((chunks, 3)),
+            pltpu.SemaphoreType.DMA((chunks, 4)),
         ],
         compiler_params=params(1),
+        cost_estimate=cost(30),
         name="dense",
     )(
         partial.reshape(groups, quarter, columns),
@@ -595,27 +744,34 @@
     )
 
     inv_root = 1.0 / (vertices * domains) ** 0.5
-    grad_self, grad_neigh = lax.psum((self_term, neigh_term), ("dom", "tile"))
-
-    back_local, back_halo, back_hub = pl.pallas_call(
+    inside = term_rows % (8 * domains) == 0
+    piece = pltpu.VMEM((domains, max(term_rows // domains, 8), outs), F32)
+
+    back_local, back_halo, back_hub, activated = pl.pallas_call(
         backward_kernel,
         out_shape=(
             shape((nl, size, columns), BF),
             shape((nh, size, columns), BF),
             shape((nb, size, columns), BF),
+            shape((quarter, outs), BF),
         ),
-        in_specs=[VMEM, SMEM, SMEM, VMEM],
-        out_specs=(VMEM,) * 3,
-        scratch_shapes=[pltpu.VMEM((nl + nh + nb, size, columns), F32)],
+        in_specs=[VMEM, SMEM, SMEM, VMEM, ANY],
+        out_specs=(VMEM,) * 3 + (ANY,),
+        scratch_shapes=[
+            pltpu.VMEM((nl + nh + nb, size, columns), F32),
+            pltpu.SemaphoreType.DMA,
+        ],
+        cost_estimate=cost(12),
         compiler_params=pltpu.CompilerParams(vmem_limit_bytes=LIMIT),
         name="backward",
-    )(edge_tiles, tile_dst, tile_src, grad_all.reshape(nl, size, columns))
-
-    grad_features = pl.pallas_call(
-        functools.partial(return_kernel, domains),
-        out_shape=shape((quarter, columns), BF),
-        in_specs=[VMEM] * 7,
-        out_specs=VMEM,
+    )(edge_tiles, tile_dst, tile_src, grad_all.reshape(nl, size, columns), activated)
+
+    term_shape = (term_rows, outs)
+    grad_features, total = pl.pallas_call(
+        functools.partial(return_kernel, domains, inside, inv_root),
+        out_shape=(shape((quarter, columns), BF), shape((groups,) + term_shape, F32)),
+        in_specs=[VMEM] * 8,
+        out_specs=(VMEM, VMEM),
         scratch_shapes=[
             pltpu.VMEM((2, quarter, columns), BF),
             block,
@@ -630,6 +786,14 @@
             pltpu.VMEM((count, hub_own, columns), BF),
             pltpu.VMEM((domains, per_peer, columns), BF),
             pltpu.VMEM((domains, hub_own, columns), BF),
+            pltpu.VMEM((2,) + term_shape, BF),
+            pltpu.VMEM(term_shape, BF),
+            pltpu.VMEM(term_shape, BF),
+            piece,
+            piece,
+            pltpu.VMEM(piece.shape[1:], F32),
+            piece,
+            pltpu.VMEM(term_shape, F32),
             pltpu.VMEM((quarter, columns), F32),
             sem(2),
             sem(2),
@@ -640,8 +804,13 @@
         + [sem(count)] * 4
         + [sem(count)] * 2
         + [sem(domains)] * 2
-        + [sem(domains)] * 4,
+        + [sem(domains)] * 4
+        + [sem(2)] * 2
+        + [sem(1)] * 2
+        + [sem(domains)] * 4
+        + [sem(3), sem(4)],
         compiler_params=params(2),
+        cost_estimate=cost(30),
         name="give_back",
     )(
         back_local.reshape(groups, quarter, columns),
@@ -651,8 +820,12 @@
         hub_row,
         grad_hidden,
         self_weight,
+        terms,
     )
-    return activated, grad_features, grad_self * inv_root, grad_neigh * inv_root
+    if not inside:
+        total = lax.psum(total, ("dom", "tile")) * inv_root
+    both = total.reshape(2, columns, outs)
+    return activated, grad_features, both[0], both[1]
 
 
 def solution(mesh):

time: 206 us -> 88.5 us (0.43)
  waiting for transfers between devices: 99.8 us -> 0 us
  between operations: 14.2 us -> 0.77 us
  local copies, waits for them, and re-layouts: 9.5 us -> 3.85 us
  Pallas kernels: 80.4 us -> 83.6 us
    psum x1 -> x0, waiting for transfers between devices: 99.8 us -> none  [on_device(): grad_self, grad_neigh = lax.psum((self_term, neigh_term), ('dom', 'tile'))]
    unnamed x42 -> x21, local copies, waits for them, and re-layouts: 9.5 us -> 3.02 us
    pallas_call x1, Pallas kernels: 24.2 us -> 29.7 us  [on_device(): pl.pallas_call(functools.partial(return_kernel, domains, inside, inv_root...]
  transfers between devices with their start and end apart: 1 -> 0, of which waited for: 1 -> 0; matrix products, arithmetic and copies ran while one was open for 0% -> 0% of each run, Pallas kernels for 15% -> 0%
where the time goes in v2:
time: 88.5 us; the launch traced here: 88.3 us
  Pallas kernels  83.6 us (94%)
  local copies, waits for them, and re-layouts  3.85 us (4%)
    pallas_call x1, Pallas kernels, on_device(): pl.pallas_call(functools.partial(return_kernel, domains, inside, inv_root...  29.7 us
    pallas_call x1, Pallas kernels, on_device(): pl.pallas_call(functools.partial(collect_kernel, domains), out_shape=(sha...  25.2 us
    pallas_call x1, Pallas kernels, on_device(): pl.pallas_call(functools.partial(dense_kernel, domains), out_shape=(shape...  17 us
    pallas_call x1, Pallas kernels, on_device(): pl.pallas_call(forward_kernel, out_shape=(shape((nl, size, columns), BF),...  6.08 us
    pallas_call x1, Pallas kernels, on_device(): pl.pallas_call(backward_kernel, out_shape=(shape((nl, size, columns), BF)...  5.71 us
    unnamed x21, local copies, waits for them, and re-layouts  3.02 us

profile of v2, /device:TPU:0, one launch (start us, length us, event | category | flops | bytes accessed | tf_op | source)
XLA Modules:
  0.0 88.3 jit_solution(12181934413611370262)
XLA Ops:
  0.6 0.0 copy-start.3
  0.6 0.9 %copy-done.3 = bf16[512,256]{1,0:T(8,128)(2,1)S(1)} copy-done((bf16[512,256]{1,0:T(8,128)(2,1)S(1)}, bf16[512,256]{1,0:T(8,128)(2,1)}, u32[]{:S(2)}) %copy-start.3) | copy-done | bytes 262168
  1.6 0.0 copy-start.7
  1.6 0.7 copy-done.7
  2.3 0.0 copy-start.9
  2.3 0.7 copy-done.9
  2.9 25.2 %collect.1 = (bf16[4,512,256]{2,1,0:T(8,128)(2,1)S(1)}, bf16[8,128,256]{2,1,0:T(8,128)(2,1)S(1)}, bf16[8,32,256]{2,1,0:T(8,128)(2,1)S(1)}) custom-call(bf16[512,256]{1,0:T(8,128)(2,1)S(1)} %copy-done.3, s32[8,1,128]{2,1,0:T(1,128)S(1)} %bitcast.18, s32[1,32]{1,0:T(1,128)S(1)} %bitcast.20), custom_call_target="tpu_custom_call" | custom-call | flops 2013265920 | bytes 31457280 | tf_op jit(solution)/shard_map/collect/pallas_call | solution.py:657
  28.2 0.0 copy-start.4
  28.2 0.0 copy-start.5
  28.2 0.0 copy-start.6
  28.2 0.0 copy-done
  28.2 0.0 copy-done.1
  28.2 0.0 copy-done.2
  28.2 6.1 %aggregate.1 = (bf16[16,128,256]{2,1,0:T(8,128)(2,1)S(1)}, f32[16,8,128]{2,1,0:T(8,128)S(1)}) custom-call(bf16[72,128,128]{2,1,0:T(8,128)(2,1)S(1)} %copy-done, s32[72]{0:T(128)S(1)} %copy-done.1, s32[72]{0:T(128)S(1)} %copy-done.2, bf16[16,128,256]{2,1,0:T(8,128)(2,1)S(1)} %bitcast.11, bf16[8,128,256]{2,1,0:T(8,128)(2,1)S(1)} %get-tuple-element.20.halo, ...), custom_call_target="tpu_custom_call" | custom-call | flops 805306368 | bytes 12582912 | tf_op jit(solution)/shard_map/aggregate/pallas_call | solution.py:682
  34.3 0.0 copy-done.4
  34.3 0.0 copy-done.5
  34.3 0.0 copy-done.6
  34.3 17.0 %dense.1 = (bf16[512,256]{1,0:T(8,128)(2,1)S(1)}, bf16[512,256]{1,0:T(8,128)(2,1)S(1)}, bf16[4,2,256,256]{3,2,1,0:T(8,128)(2,1)S(1)}, bf16[4,128,256]{2,1,0:T(8,128)(2,1)S(1)}) custom-call(bf16[4,512,256]{2,1,0:T(8,128)(2,1)S(1)} %bitcast.15, f32[4,4,8,128]{3,2,1,0:T(8,128)S(1)} %bitcast.17, bf16[512,256]{1,0:T(8,128)(2,1)S(1)} %copy-done.3, ...), custom_call_target="tpu_custom_call" | custom-call | flops 2013265920 | bytes 31457280 | tf_op jit(solution)/shard_map/dense/pallas_call | solution.py:708
  51.3 0.0 copy-start.8
  51.3 5.7 %backward.1 = (bf16[16,128,256]{2,1,0:T(8,128)(2,1)S(1)}, bf16[8,128,256]{2,1,0:T(8,128)(2,1)S(1)}, bf16[2,128,256]{2,1,0:T(8,128)(2,1)S(1)}, bf16[512,256]{1,0:T(8,128)(2,1)}) custom-call(bf16[72,128,128]{2,1,0:T(8,128)(2,1)S(1)} %copy-done, s32[72]{0:T(128)S(1)} %copy-done.1, s32[72]{0:T(128)S(1)} %copy-done.2, bf16[16,128,256]{2,1,0:T(8,128)(2,1)S(1)} %bitcast.12, ...), custom_call_target="tpu_custom_call" | custom-call | flops 805306368 | bytes 12582912 | tf_op jit(solution)/shard_map/backward/pallas_call | solution.py:750
  57.1 0.0 copy-done.8
  57.1 29.7 %give_back.1 = (bf16[512,256]{1,0:T(8,128)(2,1)S(1)}, f32[4,128,256]{2,1,0:T(8,128)S(1)}) custom-call(bf16[4,512,256]{2,1,0:T(8,128)(2,1)S(1)} %bitcast.14, bf16[8,128,256]{2,1,0:T(8,128)(2,1)S(1)} %get-tuple-element.28.halo, bf16[8,32,256]{2,1,0:T(8,128)(2,1)S(1)} %bitcast.16, s32[8,1,128]{2,1,0:T(1,128)S(1)} %bitcast.19, s32[1,32]{1,0:T(1,128)S(1)} %bitcast.21, ...), custom_call_target="tpu_custom_call" | custom-call | flops 2013265920 | bytes 31457280 | tf_op jit(solution)/shard_map/give_back/pallas_call | solution.py:770
  86.7 0.8 fusion
  87.6 0.7 copy.14
  (3 shorter events, 0.0 us)
Async XLA Ops:
  0.6 1.0 %copy-start.3 = (bf16[512,256]{1,0:T(8,128)(2,1)S(1)}, bf16[512,256]{1,0:T(8,128)(2,1)}, u32[]{:S(2)}) copy-start(bf16[512,256]{1,0:T(8,128)(2,1)} %feat.3) | copy-start | bytes 786436
  1.6 0.7 copy-start.7
  2.3 0.7 copy-start.9
  2.9 25.3 %copy-start = (bf16[72,128,128]{2,1,0:T(8,128)(2,1)S(1)}, bf16[72,128,128]{2,1,0:T(8,128)(2,1)}, u32[]{:S(2)}) copy-start(bf16[72,128,128]{2,1,0:T(8,128)(2,1)} %tiles.3) | copy-start | bytes 7077892
  2.9 25.3 %copy-start.1 = (s32[72]{0:T(128)S(1)}, s32[72]{0:T(128)}, u32[]{:S(2)}) copy-start(s32[72]{0:T(128)} %dst.3) | copy-start | bytes 868
  2.9 25.3 %copy-start.2 = (s32[72]{0:T(128)S(1)}, s32[72]{0:T(128)}, u32[]{:S(2)}) copy-start(s32[72]{0:T(128)} %src.3) | copy-start | bytes 868
  28.2 6.2 %copy-start.4 = (bf16[512,256]{1,0:T(8,128)(2,1)S(1)}, bf16[512,256]{1,0:T(8,128)(2,1)}, u32[]{:S(2)}) copy-start(bf16[512,256]{1,0:T(8,128)(2,1)} %grad_out.1) | copy-start | bytes 786436
  28.2 6.2 %copy-start.5 = (bf16[256,256]{1,0:T(8,128)(2,1)S(1)}, bf16[256,256]{1,0:T(8,128)(2,1)}, u32[]{:S(2)}) copy-start(bf16[256,256]{1,0:T(8,128)(2,1)} %neigh_weight.1) | copy-start | bytes 393220
  28.2 6.2 %copy-start.6 = (bf16[256,256]{1,0:T(8,128)(2,1)S(1)}, bf16[256,256]{1,0:T(8,128)(2,1)}, u32[]{:S(2)}) copy-start(bf16[256,256]{1,0:T(8,128)(2,1)} %self_weight.3) | copy-start | bytes 393220
  51.3 5.7 %copy-start.8 = (s32[1,1024]{1,0:T(1,128)S(1)}, s32[1,1024]{1,0:T(1,128)}, u32[]{:S(2)}) copy-start(s32[1,1024]{1,0:T(1,128)} %param.16) | copy-start | bytes 12292

commit v3 on v2

--- a/solution.py
+++ b/solution.py
@@ -74,9 +74,11 @@
         lax.fori_loop(0, count, step, 0)
 
 
-def dom_send(count, me, own_slots, pairs):
+def dom_send(count, me, own_slots, pairs, ready=None):
     def body(i):
         there = own_slots(i)
+        if ready is not None:
+            ready(i)
         for staged, landing, send, recv in pairs:
 
             @pl.when(there != me)
@@ -90,7 +92,7 @@
     each(count, body)
 
 
-def dom_gather(count, me, t, core, across, diagonal, slots, pairs, forward):
+def dom_gather(count, me, t, core, across, diagonal, slots, pairs, forward, between=None):
     mine, theirs = slots(t), slots(across)
 
     def first(i):
@@ -108,6 +110,8 @@
             remote(spot, spot, fcore.at[there], recv.at[there], tile=core).start()
 
     each(count, first)
+    if between is not None:
+        between()
 
     def second(i):
         there = theirs(i)
@@ -189,20 +193,20 @@
     tile_gather_start(feat, local, t, core, across, tile_send, tile_recv)
     local[t] = feat[...]
 
+    def term(ids, part, values):
+        spot = lax.broadcasted_iota(jnp.int32, (quarter, ids.shape[1]), 0) + part * quarter
+        chosen = (spot == ids).astype(F32).astype(BF)
+        return lax.dot_general(chosen, values, TN, preferred_element_type=F32)
+
     def add(part, source, first):
         values = source[...]
 
-        def term(ids):
-            spot = lax.broadcasted_iota(jnp.int32, (quarter, ids.shape[1]), 0) + part * quarter
-            chosen = (spot == ids).astype(F32).astype(BF)
-            return lax.dot_general(chosen, values, TN, preferred_element_type=F32)
-
         def body(i):
-            found = term(halo_ids[mine(i)])
+            found = term(halo_ids[mine(i)], part, values)
             halo_acc[i] = found if first else halo_acc[i] + found
 
         each(count, body)
-        found = term(hub_ids[...])
+        found = term(hub_ids[...], part, values)
         hub_acc[...] = found if first else hub_acc[...] + found
 
     add(t, feat, True)
@@ -211,17 +215,16 @@
     tile_gather_middle(local, core, across, tile_send, tile_recv)
     add(across, local.at[across], False)
     remote(feat, local.at[diagonal], tile_send.at[2], tile_recv.at[diagonal], tile=core).wait_recv()
-    add(diagonal, local.at[diagonal], False)
-    own_hubs = hub_acc[...].astype(BF)
-
-    def body(i):
+    last = local[diagonal]
+    own_hubs = (hub_acc[...] + term(hub_ids[...], diagonal, last)).astype(BF)
+
+    def ready(i):
         staged_hub[i] = own_hubs
-        staged_halo[i] = halo_acc[i].astype(BF)
-
-    each(count, body)
+        staged_halo[i] = (halo_acc[i] + term(halo_ids[mine(i)], diagonal, last)).astype(BF)
+
     pairs = ((staged_halo, halo, halo_send, halo_recv), (staged_hub, hub, hub_send, hub_recv))
     forward = ((halo_core, halo_across), (hub_core, hub_across))
-    dom_send(count, me, mine, pairs)
+    dom_send(count, me, mine, pairs, ready)
     dom_gather(count, me, t, core, across, diagonal, slots, pairs, forward)
     tile_gather_sent(feat, local, core, across, tile_send, tile_recv)
 
@@ -240,7 +243,7 @@
     ones = jnp.ones((8, tiles.shape[2]), BF)
     for copy in copies:
         copy.wait()
-    step = 4
+    step = 8 if tiles.shape[0] % 8 == 0 else 1
 
     def body(k, carry):
         found = []
@@ -268,7 +271,7 @@
     passing.start()
     nl, nh = local.shape[0], halo.shape[0]
     acc[...] = jnp.zeros_like(acc)
-    step = 4
+    step = 8 if tiles.shape[0] % 8 == 0 else 1
 
     def body(k, carry):
         found = []
@@ -433,6 +436,7 @@
     term_sum,
     term_ag,
     term_mine,
+    term_land,
     acc,
     pair_sems,
     pair_recv,
@@ -539,7 +543,7 @@
         term_second.wait_recv()
         term_cross.wait_recv()
         cut = terms[t].astype(F32) + term_in[0].astype(F32) + term_other[...].astype(F32)
-        term_cut[...] = cut.reshape(term_cut.shape)
+        term_cut[...] = cut.reshape(term_cut.shape).astype(BF)
 
         def to_all(source, landed, send, recv, start):
             for p in range(domains):
@@ -566,17 +570,21 @@
     second = remote(local.at[core], landing.at[0], pair_sems.at[0], pair_recv.at[0], tile=core)
     second.wait_recv()
     acc[...] += local[t].astype(F32) + landing[0].astype(F32)
-    if inside:
+
+    def between():
         to_all(*scatter, False)
-        term_sum[...] = jnp.sum(term_rs[...], axis=0) * inv_root
+        term_sum[...] = (jnp.sum(term_rs[...].astype(F32), axis=0) * inv_root).astype(BF)
         to_all(*collect, True)
         term_ag[me] = term_sum[...]
-    dom_gather(count, me, t, core, across, diagonal, slots, pairs, forward)
+
+    dom_gather(
+        count, me, t, core, across, diagonal, slots, pairs, forward, between if inside else None
+    )
     if inside:
         to_all(*collect, False)
-        term_mine[...] = term_ag[...].reshape(term_mine.shape)
-        tile_gather_start(term_mine, term_out, t, core, across, term_tsend, term_trecv)
-        term_out[t] = term_mine[...]
+        term_mine[...] = term_ag[...].astype(F32).reshape(term_mine.shape).astype(BF)
+        tile_gather_start(term_mine, term_land, t, core, across, term_tsend, term_trecv)
+        term_land[t] = term_mine[...]
 
     def pick(ids):
         spot = lax.broadcasted_iota(jnp.int32, (quarter, ids.shape[1]), 0) + t * quarter
@@ -594,13 +602,14 @@
     cross.wait_recv()
     out[...] = (acc[...] + other[...].astype(F32)).astype(BF)
     if inside:
-        tile_gather_middle(term_out, core, across, term_tsend, term_trecv)
-        tile_gather_end(term_mine, term_out, core, across, diagonal, term_tsend, term_trecv)
+        tile_gather_middle(term_land, core, across, term_tsend, term_trecv)
+        tile_gather_end(term_mine, term_land, core, across, diagonal, term_tsend, term_trecv)
         term_first.wait_send()
         term_second.wait_send()
         term_cross.wait_send()
         all_sent(*scatter)
         all_sent(*collect)
+        term_out[...] = term_land[...].astype(F32)
     else:
         term_out[...] = terms[...].astype(F32)
     first.wait_send()
@@ -701,7 +710,7 @@
         hub.reshape(nb, size, columns),
     )
 
-    chunks = 2
+    chunks = 4
     block = pltpu.VMEM((quarter, columns), BF)
     part = pltpu.VMEM((chunks, quarter // chunks, columns), BF)
     term_rows = 2 * columns // groups
@@ -744,8 +753,8 @@
     )
 
     inv_root = 1.0 / (vertices * domains) ** 0.5
-    inside = term_rows % (8 * domains) == 0
-    piece = pltpu.VMEM((domains, max(term_rows // domains, 8), outs), F32)
+    inside = term_rows % (16 * domains) == 0
+    piece = pltpu.VMEM((domains, max(term_rows // domains, 16), outs), BF)
 
     back_local, back_halo, back_hub, activated = pl.pallas_call(
         backward_kernel,
@@ -791,9 +800,10 @@
             pltpu.VMEM(term_shape, BF),
             piece,
             piece,
-            pltpu.VMEM(piece.shape[1:], F32),
+            pltpu.VMEM(piece.shape[1:], BF),
             piece,
-            pltpu.VMEM(term_shape, F32),
+            pltpu.VMEM(term_shape, BF),
+            pltpu.VMEM((groups,) + term_shape, BF),
             pltpu.VMEM((quarter, columns), F32),
             sem(2),
             sem(2),

time: 88.5 us -> 83.4 us (0.942)
  Pallas kernels: 83.6 us -> 78.6 us
    pallas_call x1, Pallas kernels: 29.7 us -> 27.5 us  [on_device(): pl.pallas_call(functools.partial(return_kernel, domains, inside, inv_root...]
    pallas_call x1, Pallas kernels: 5.71 us -> 3.97 us  [on_device(): pl.pallas_call(backward_kernel, out_shape=(shape((nl, size, columns), BF)...]
    pallas_call x1, Pallas kernels: 6.08 us -> 4.83 us  [on_device(): pl.pallas_call(forward_kernel, out_shape=(shape((nl, size, columns), BF),...]
where the time goes in v3:
time: 83.4 us; the launch traced here: 83.2 us
  Pallas kernels  78.6 us (94%)
  local copies, waits for them, and re-layouts  3.85 us (5%)
    pallas_call x1, Pallas kernels, on_device(): pl.pallas_call(functools.partial(return_kernel, domains, inside, inv_root...  27.5 us
    pallas_call x1, Pallas kernels, on_device(): pl.pallas_call(functools.partial(collect_kernel, domains), out_shape=(sha...  25.3 us
    pallas_call x1, Pallas kernels, on_device(): pl.pallas_call(functools.partial(dense_kernel, domains), out_shape=(shape...  17 us
    pallas_call x1, Pallas kernels, on_device(): pl.pallas_call(forward_kernel, out_shape=(shape((nl, size, columns), BF),...  4.83 us
    pallas_call x1, Pallas kernels, on_device(): pl.pallas_call(backward_kernel, out_shape=(shape((nl, size, columns), BF)...  3.97 us
    unnamed x21, local copies, waits for them, and re-layouts  3.02 us

profile of v3, /device:TPU:0, one launch (start us, length us, event | category | flops | bytes accessed | tf_op | source)
XLA Modules:
  0.0 83.2 jit_solution(9587334607558781956)
XLA Ops:
  0.6 0.0 copy-start.3
  0.6 0.9 %copy-done.3 = bf16[512,256]{1,0:T(8,128)(2,1)S(1)} copy-done((bf16[512,256]{1,0:T(8,128)(2,1)S(1)}, bf16[512,256]{1,0:T(8,128)(2,1)}, u32[]{:S(2)}) %copy-start.3) | copy-done | bytes 262168
  1.6 0.0 copy-start.7
  1.6 0.7 copy-done.7
  2.3 0.0 copy-start.9
  2.3 0.7 copy-done.9
  2.9 25.3 %collect.1 = (bf16[4,512,256]{2,1,0:T(8,128)(2,1)S(1)}, bf16[8,128,256]{2,1,0:T(8,128)(2,1)S(1)}, bf16[8,32,256]{2,1,0:T(8,128)(2,1)S(1)}) custom-call(bf16[512,256]{1,0:T(8,128)(2,1)S(1)} %copy-done.3, s32[8,1,128]{2,1,0:T(1,128)S(1)} %bitcast.18, s32[1,32]{1,0:T(1,128)S(1)} %bitcast.20), custom_call_target="tpu_custom_call" | custom-call | flops 2013265920 | bytes 31457280 | tf_op jit(solution)/shard_map/collect/pallas_call | solution.py:666
  28.2 0.0 copy-start.4
  28.2 0.0 copy-start.5
  28.2 0.0 copy-start.6
  28.2 0.0 copy-done
  28.2 0.0 copy-done.1
  28.2 0.0 copy-done.2
  28.3 4.8 %aggregate.1 = (bf16[16,128,256]{2,1,0:T(8,128)(2,1)S(1)}, f32[16,8,128]{2,1,0:T(8,128)S(1)}) custom-call(bf16[72,128,128]{2,1,0:T(8,128)(2,1)S(1)} %copy-done, s32[72]{0:T(128)S(1)} %copy-done.1, s32[72]{0:T(128)S(1)} %copy-done.2, bf16[16,128,256]{2,1,0:T(8,128)(2,1)S(1)} %bitcast.11, bf16[8,128,256]{2,1,0:T(8,128)(2,1)S(1)} %get-tuple-element.20.halo, ...), custom_call_target="tpu_custom_call" | custom-call | flops 805306368 | bytes 12582912 | tf_op jit(solution)/shard_map/aggregate/pallas_call | solution.py:691
  33.1 0.0 copy-done.4
  33.1 0.0 copy-done.5
  33.1 0.0 copy-done.6
  33.1 17.0 %dense.1 = (bf16[512,256]{1,0:T(8,128)(2,1)S(1)}, bf16[512,256]{1,0:T(8,128)(2,1)S(1)}, bf16[4,4,128,256]{3,2,1,0:T(8,128)(2,1)S(1)}, bf16[4,128,256]{2,1,0:T(8,128)(2,1)S(1)}) custom-call(bf16[4,512,256]{2,1,0:T(8,128)(2,1)S(1)} %bitcast.15, f32[4,4,8,128]{3,2,1,0:T(8,128)S(1)} %bitcast.17, bf16[512,256]{1,0:T(8,128)(2,1)S(1)} %copy-done.3, ...), custom_call_target="tpu_custom_call" | custom-call | flops 2013265920 | bytes 31457280 | tf_op jit(solution)/shard_map/dense/pallas_call | solution.py:717
  50.2 0.0 copy-start.8
  50.2 4.0 %backward.1 = (bf16[16,128,256]{2,1,0:T(8,128)(2,1)S(1)}, bf16[8,128,256]{2,1,0:T(8,128)(2,1)S(1)}, bf16[2,128,256]{2,1,0:T(8,128)(2,1)S(1)}, bf16[512,256]{1,0:T(8,128)(2,1)}) custom-call(bf16[72,128,128]{2,1,0:T(8,128)(2,1)S(1)} %copy-done, s32[72]{0:T(128)S(1)} %copy-done.1, s32[72]{0:T(128)S(1)} %copy-done.2, bf16[16,128,256]{2,1,0:T(8,128)(2,1)S(1)} %bitcast.12, ...), custom_call_target="tpu_custom_call" | custom-call | flops 805306368 | bytes 12582912 | tf_op jit(solution)/shard_map/backward/pallas_call | solution.py:759
  54.2 0.0 copy-done.8
  54.2 27.5 %give_back.1 = (bf16[512,256]{1,0:T(8,128)(2,1)S(1)}, f32[4,128,256]{2,1,0:T(8,128)S(1)}) custom-call(bf16[4,512,256]{2,1,0:T(8,128)(2,1)S(1)} %bitcast.14, bf16[8,128,256]{2,1,0:T(8,128)(2,1)S(1)} %get-tuple-element.28.halo, bf16[8,32,256]{2,1,0:T(8,128)(2,1)S(1)} %bitcast.16, s32[8,1,128]{2,1,0:T(1,128)S(1)} %bitcast.19, s32[1,32]{1,0:T(1,128)S(1)} %bitcast.21, ...), custom_call_target="tpu_custom_call" | custom-call | flops 2013265920 | bytes 31457280 | tf_op jit(solution)/shard_map/give_back/pallas_call | solution.py:779
  81.7 0.8 fusion
  82.5 0.7 copy.14
  (3 shorter events, 0.0 us)
Async XLA Ops:
  0.6 1.0 %copy-start.3 = (bf16[512,256]{1,0:T(8,128)(2,1)S(1)}, bf16[512,256]{1,0:T(8,128)(2,1)}, u32[]{:S(2)}) copy-start(bf16[512,256]{1,0:T(8,128)(2,1)} %feat.3) | copy-start | bytes 786436
  1.6 0.7 copy-start.7
  2.3 0.7 copy-start.9
  2.9 25.3 %copy-start = (bf16[72,128,128]{2,1,0:T(8,128)(2,1)S(1)}, bf16[72,128,128]{2,1,0:T(8,128)(2,1)}, u32[]{:S(2)}) copy-start(bf16[72,128,128]{2,1,0:T(8,128)(2,1)} %tiles.3) | copy-start | bytes 7077892
  2.9 25.3 %copy-start.1 = (s32[72]{0:T(128)S(1)}, s32[72]{0:T(128)}, u32[]{:S(2)}) copy-start(s32[72]{0:T(128)} %dst.3) | copy-start | bytes 868
  2.9 25.3 %copy-start.2 = (s32[72]{0:T(128)S(1)}, s32[72]{0:T(128)}, u32[]{:S(2)}) copy-start(s32[72]{0:T(128)} %src.3) | copy-start | bytes 868
  28.2 4.9 %copy-start.4 = (bf16[512,256]{1,0:T(8,128)(2,1)S(1)}, bf16[512,256]{1,0:T(8,128)(2,1)}, u32[]{:S(2)}) copy-start(bf16[512,256]{1,0:T(8,128)(2,1)} %grad_out.1) | copy-start | bytes 786436
  28.2 4.9 %copy-start.5 = (bf16[256,256]{1,0:T(8,128)(2,1)S(1)}, bf16[256,256]{1,0:T(8,128)(2,1)}, u32[]{:S(2)}) copy-start(bf16[256,256]{1,0:T(8,128)(2,1)} %neigh_weight.1) | copy-start | bytes 393220
  28.2 4.9 %copy-start.6 = (bf16[256,256]{1,0:T(8,128)(2,1)S(1)}, bf16[256,256]{1,0:T(8,128)(2,1)}, u32[]{:S(2)}) copy-start(bf16[256,256]{1,0:T(8,128)(2,1)} %self_weight.3) | copy-start | bytes 393220
  50.2 4.0 %copy-start.8 = (s32[1,1024]{1,0:T(1,128)S(1)}, s32[1,1024]{1,0:T(1,128)}, u32[]{:S(2)}) copy-start(s32[1,1024]{1,0:T(1,128)} %param.16) | copy-start | bytes 12292

commit v4 on v3

--- a/solution.py
+++ b/solution.py
@@ -165,11 +165,14 @@
 def collect_kernel(
     domains,
     feat,
-    halo_ids,
-    hub_ids,
+    halo_table,
+    hub_table,
     local,
     halo,
     hub,
+    halo_ids,
+    hub_ids,
+    id_sems,
     staged_halo,
     staged_hub,
     halo_acc,
@@ -189,6 +192,10 @@
     me, t, core, across, diagonal, slots = places(domains)
     mine = slots(t)
     quarter = feat.shape[0]
+    halo_copy = pltpu.make_async_copy(halo_table, halo_ids, id_sems.at[0])
+    hub_copy = pltpu.make_async_copy(hub_table, hub_ids, id_sems.at[1])
+    halo_copy.start()
+    hub_copy.start()
     greet(me, (core, across, diagonal), mine, count, met(me, mine, domains))
     tile_gather_start(feat, local, t, core, across, tile_send, tile_recv)
     local[t] = feat[...]
@@ -209,6 +216,8 @@
         found = term(hub_ids[...], part, values)
         hub_acc[...] = found if first else hub_acc[...] + found
 
+    halo_copy.wait()
+    hub_copy.wait()
     add(t, feat, True)
     remote(feat, local.at[core], tile_send.at[1], tile_recv.at[core], tile=core).wait_recv()
     add(core, local.at[core], False)
@@ -243,7 +252,7 @@
     ones = jnp.ones((8, tiles.shape[2]), BF)
     for copy in copies:
         copy.wait()
-    step = 8 if tiles.shape[0] % 8 == 0 else 1
+    step = 24 if tiles.shape[0] % 24 == 0 else 1
 
     def body(k, carry):
         found = []
@@ -271,7 +280,7 @@
     passing.start()
     nl, nh = local.shape[0], halo.shape[0]
     acc[...] = jnp.zeros_like(acc)
-    step = 8 if tiles.shape[0] % 8 == 0 else 1
+    step = 24 if tiles.shape[0] % 24 == 0 else 1
 
     def body(k, carry):
         found = []
@@ -670,9 +679,12 @@
             shape((domains, per_peer, columns), BF),
             shape((domains, hub_own, columns), BF),
         ),
-        in_specs=[VMEM] * 3,
+        in_specs=[VMEM, ANY, ANY],
         out_specs=(VMEM,) * 3,
         scratch_shapes=[
+            pltpu.VMEM((domains, 1, per_peer), jnp.int32),
+            pltpu.VMEM((1, hub_own), jnp.int32),
+            sem(2),
             pltpu.VMEM((count, per_peer, columns), BF),
             pltpu.VMEM((count, hub_own, columns), BF),
             pltpu.VMEM((count, per_peer, columns), F32),

time: 83.4 us -> 81.4 us (0.976)
  Pallas kernels: 78.6 us -> 76.6 us
    pallas_call x1, Pallas kernels: 3.97 us -> 2.86 us  [on_device(): pl.pallas_call(backward_kernel, out_shape=(shape((nl, size, columns), BF)...]
    pallas_call x1, Pallas kernels: 4.83 us -> 3.98 us  [on_device(): pl.pallas_call(forward_kernel, out_shape=(shape((nl, size, columns), BF),...]
where the time goes in v4:
time: 81.4 us; the launch traced here: 81.3 us
  Pallas kernels  76.6 us (94%)
  local copies, waits for them, and re-layouts  3.85 us (5%)
    pallas_call x1, Pallas kernels, on_device(): pl.pallas_call(functools.partial(return_kernel, domains, inside, inv_root...  27.5 us
    pallas_call x1, Pallas kernels, on_device(): pl.pallas_call(functools.partial(collect_kernel, domains), out_shape=(sha...  25.3 us
    pallas_call x1, Pallas kernels, on_device(): pl.pallas_call(functools.partial(dense_kernel, domains), out_shape=(shape...  17 us
    pallas_call x1, Pallas kernels, on_device(): pl.pallas_call(forward_kernel, out_shape=(shape((nl, size, columns), BF),...  3.98 us
    unnamed x21, local copies, waits for them, and re-layouts  3.02 us
    pallas_call x1, Pallas kernels, on_device(): pl.pallas_call(backward_kernel, out_shape=(shape((nl, size, columns), BF)...  2.86 us

profile of v4, /device:TPU:0, one launch (start us, length us, event | category | flops | bytes accessed | tf_op | source)
XLA Modules:
  0.0 81.3 jit_solution(10232735231567808321)
XLA Ops:
  0.6 0.0 copy-start.3
  0.6 0.9 %copy-done.3 = bf16[512,256]{1,0:T(8,128)(2,1)S(1)} copy-done((bf16[512,256]{1,0:T(8,128)(2,1)S(1)}, bf16[512,256]{1,0:T(8,128)(2,1)}, u32[]{:S(2)}) %copy-start.3) | copy-done | bytes 262168
  1.6 0.0 copy-start.7
  1.6 0.7 copy-done.7
  2.3 0.0 copy-start.9
  2.3 0.7 copy-done.9
  2.9 25.3 %collect.1 = (bf16[4,512,256]{2,1,0:T(8,128)(2,1)S(1)}, bf16[8,128,256]{2,1,0:T(8,128)(2,1)S(1)}, bf16[8,32,256]{2,1,0:T(8,128)(2,1)S(1)}) custom-call(bf16[512,256]{1,0:T(8,128)(2,1)S(1)} %copy-done.3, s32[8,1,128]{2,1,0:T(1,128)S(1)} %bitcast.18, s32[1,32]{1,0:T(1,128)S(1)} %bitcast.20), custom_call_target="tpu_custom_call" | custom-call | flops 2013265920 | bytes 31457280 | tf_op jit(solution)/shard_map/collect/pallas_call | solution.py:675
  28.2 0.0 copy-start.4
  28.2 0.0 copy-start.5
  28.2 0.0 copy-start.6
  28.3 0.0 copy-done
  28.3 0.0 copy-done.1
  28.3 0.0 copy-done.2
  28.3 4.0 %aggregate.1 = (bf16[16,128,256]{2,1,0:T(8,128)(2,1)S(1)}, f32[16,8,128]{2,1,0:T(8,128)S(1)}) custom-call(bf16[72,128,128]{2,1,0:T(8,128)(2,1)S(1)} %copy-done, s32[72]{0:T(128)S(1)} %copy-done.1, s32[72]{0:T(128)S(1)} %copy-done.2, bf16[16,128,256]{2,1,0:T(8,128)(2,1)S(1)} %bitcast.11, bf16[8,128,256]{2,1,0:T(8,128)(2,1)S(1)} %get-tuple-element.20.halo, ...), custom_call_target="tpu_custom_call" | custom-call | flops 805306368 | bytes 12582912 | tf_op jit(solution)/shard_map/aggregate/pallas_call | solution.py:703
  32.3 0.0 copy-done.4
  32.3 0.0 copy-done.5
  32.3 0.0 copy-done.6
  32.3 17.0 %dense.1 = (bf16[512,256]{1,0:T(8,128)(2,1)S(1)}, bf16[512,256]{1,0:T(8,128)(2,1)S(1)}, bf16[4,4,128,256]{3,2,1,0:T(8,128)(2,1)S(1)}, bf16[4,128,256]{2,1,0:T(8,128)(2,1)S(1)}) custom-call(bf16[4,512,256]{2,1,0:T(8,128)(2,1)S(1)} %bitcast.15, f32[4,4,8,128]{3,2,1,0:T(8,128)S(1)} %bitcast.17, bf16[512,256]{1,0:T(8,128)(2,1)S(1)} %copy-done.3, ...), custom_call_target="tpu_custom_call" | custom-call | flops 2013265920 | bytes 31457280 | tf_op jit(solution)/shard_map/dense/pallas_call | solution.py:729
  49.3 0.0 copy-start.8
  49.3 2.9 %backward.1 = (bf16[16,128,256]{2,1,0:T(8,128)(2,1)S(1)}, bf16[8,128,256]{2,1,0:T(8,128)(2,1)S(1)}, bf16[2,128,256]{2,1,0:T(8,128)(2,1)S(1)}, bf16[512,256]{1,0:T(8,128)(2,1)}) custom-call(bf16[72,128,128]{2,1,0:T(8,128)(2,1)S(1)} %copy-done, s32[72]{0:T(128)S(1)} %copy-done.1, s32[72]{0:T(128)S(1)} %copy-done.2, bf16[16,128,256]{2,1,0:T(8,128)(2,1)S(1)} %bitcast.12, ...), custom_call_target="tpu_custom_call" | custom-call | flops 805306368 | bytes 12582912 | tf_op jit(solution)/shard_map/backward/pallas_call | solution.py:771
  52.2 0.0 copy-done.8
  52.2 27.5 %give_back.1 = (bf16[512,256]{1,0:T(8,128)(2,1)S(1)}, f32[4,128,256]{2,1,0:T(8,128)S(1)}) custom-call(bf16[4,512,256]{2,1,0:T(8,128)(2,1)S(1)} %bitcast.14, bf16[8,128,256]{2,1,0:T(8,128)(2,1)S(1)} %get-tuple-element.28.halo, bf16[8,32,256]{2,1,0:T(8,128)(2,1)S(1)} %bitcast.16, s32[8,1,128]{2,1,0:T(1,128)S(1)} %bitcast.19, s32[1,32]{1,0:T(1,128)S(1)} %bitcast.21, ...), custom_call_target="tpu_custom_call" | custom-call | flops 2013265920 | bytes 31457280 | tf_op jit(solution)/shard_map/give_back/pallas_call | solution.py:791
  79.7 0.8 %fusion = (f32[2,128,256]{2,1,0:T(8,128)}, f32[2,128,256]{2,1,0:T(8,128)}) fusion(f32[4,128,256]{2,1,0:T(8,128)S(1)} %get-tuple-element.33), kind=kLoop, calls=%fused_computation | loop fusion | bytes 1048576 | tf_op jit(solution)/shard_map/slice | solution.py:850
  80.6 0.7 copy.14
  (3 shorter events, 0.0 us)
Async XLA Ops:
  0.6 1.0 %copy-start.3 = (bf16[512,256]{1,0:T(8,128)(2,1)S(1)}, bf16[512,256]{1,0:T(8,128)(2,1)}, u32[]{:S(2)}) copy-start(bf16[512,256]{1,0:T(8,128)(2,1)} %feat.3) | copy-start | bytes 786436
  1.6 0.7 copy-start.7
  2.3 0.7 copy-start.9
  2.9 25.3 %copy-start = (bf16[72,128,128]{2,1,0:T(8,128)(2,1)S(1)}, bf16[72,128,128]{2,1,0:T(8,128)(2,1)}, u32[]{:S(2)}) copy-start(bf16[72,128,128]{2,1,0:T(8,128)(2,1)} %tiles.3) | copy-start | bytes 7077892
  2.9 25.3 %copy-start.1 = (s32[72]{0:T(128)S(1)}, s32[72]{0:T(128)}, u32[]{:S(2)}) copy-start(s32[72]{0:T(128)} %dst.3) | copy-start | bytes 868
  2.9 25.3 %copy-start.2 = (s32[72]{0:T(128)S(1)}, s32[72]{0:T(128)}, u32[]{:S(2)}) copy-start(s32[72]{0:T(128)} %src.3) | copy-start | bytes 868
  28.2 4.1 %copy-start.4 = (bf16[512,256]{1,0:T(8,128)(2,1)S(1)}, bf16[512,256]{1,0:T(8,128)(2,1)}, u32[]{:S(2)}) copy-start(bf16[512,256]{1,0:T(8,128)(2,1)} %grad_out.1) | copy-start | bytes 786436
  28.2 4.0 %copy-start.5 = (bf16[256,256]{1,0:T(8,128)(2,1)S(1)}, bf16[256,256]{1,0:T(8,128)(2,1)}, u32[]{:S(2)}) copy-start(bf16[256,256]{1,0:T(8,128)(2,1)} %neigh_weight.1) | copy-start | bytes 393220
  28.2 4.0 %copy-start.6 = (bf16[256,256]{1,0:T(8,128)(2,1)S(1)}, bf16[256,256]{1,0:T(8,128)(2,1)}, u32[]{:S(2)}) copy-start(bf16[256,256]{1,0:T(8,128)(2,1)} %self_weight.3) | copy-start | bytes 393220
  49.3 2.9 %copy-start.8 = (s32[1,1024]{1,0:T(1,128)S(1)}, s32[1,1024]{1,0:T(1,128)}, u32[]{:S(2)}) copy-start(s32[1,1024]{1,0:T(1,128)} %param.16) | copy-start | bytes 12292
